TPU v7x, 32 devices: a whole 2x2x4 slice. The times are simulated.
32 devices in a mesh: px: 8 (over z, x), py: 4 (over y, core).
Axes of the slice: x: 2, y: 2, z: 4, core: 2. Of those that a mesh axis runs over, the one named last changes fastest.
Arguments:
- counts: int32 [8], replicated, may hold values from 1 to 6, 16 in all
- coefficient: float32 [48, 4, 4096], P('px', 'py'), may hold values from 0.2 to 5
- signs: int32 [48, 4, 4096], P('px', 'py'), may hold values from 0 to 1
- basis_old: float32 [48, 4, 16, 4096], P('px', 'py'), may hold values from -8 to 8
- basis_last: float32 [48, 4, 16, 4096], P('px', 'py'), may hold values from -8 to 8
- residual_factor: float32 [16, 16], replicated, may hold values from -12 to 12
- previous_coef: float32 [32, 16], replicated, may hold values from -12 to 12
- sample_rows: int32 [2048], replicated, may hold values from 0 to 262143, as said below
Outputs:
- new_block: float32 [48, 4, 16, 4096], P('px', 'py')
- sketch: float32 [48, 2048], P(None, ('px', 'py'))
- solution: float32 [32, 16], replicated
Inputs may be any that keep to these rules, and one draw needn't show every extreme that they name: Index i of px owns counts[i] consecutive patch columns, in px order; the largest count is exactly 6. `sample_rows`: distinct cell numbers, among them 0 and 262143.
All inputs are finite; a program needn't handle non-finite values.
Results may differ from a plain program's by a relative error of at most 0.0003.
Values sent between devices are 32-bit elements; how exact they have to be, the bound alone decides.
A program may use at most 256 MiB of HBM per device.

v0:
```python
import math

import jax
import jax.numpy as jnp
from jax import lax
from jax.sharding import PartitionSpec as P

PS = 16
K = 2048
MEANX = 2
CAP = 6
CELLS = 4096


highest = lax.Precision.HIGHEST


def extended(block, sides, width):
    for axis, dim in sides:
        count = lax.axis_size(axis)
        forward = [(i, i + 1) for i in range(count - 1)]
        backward = [(target, source) for source, target in forward]
        low = lax.ppermute(
            lax.slice_in_dim(block, block.shape[dim] - width, None, axis=dim), axis, forward
        )
        high = lax.ppermute(lax.slice_in_dim(block, 0, width, axis=dim), axis, backward)
        block = jnp.concatenate([low, block, high], axis=dim)
    return block


def parity_of(values):
    folded = values
    for amount in (16, 8, 4, 2, 1):
        folded = jnp.bitwise_xor(folded, jnp.right_shift(folded, amount))
    return jnp.bitwise_and(folded, 1)


def sign_table(length):
    indices = jnp.arange(length, dtype=jnp.int32)
    parity = parity_of(jnp.bitwise_and(indices[:, None], indices[None, :]))
    return (1 - 2 * parity).astype(jnp.float32)


def transform_cells(values):
    inner_len = min(CELLS, 128)
    outer_len = CELLS // inner_len
    shaped = values.reshape(values.shape[:-1] + (outer_len, inner_len))
    shaped = jnp.einsum("sjab,bd->sjad", shaped, sign_table(inner_len), precision=highest)
    shaped = jnp.einsum("ca,sjad->sjcd", sign_table(outer_len), shaped, precision=highest)
    return shaped.reshape(values.shape)


def shift_pair(cube_vals, low_plane, high_plane, axis_pos):
    below = jnp.concatenate(
        [
            jnp.expand_dims(low_plane, axis_pos),
            lax.slice_in_dim(cube_vals, 0, PS - 1, axis=axis_pos),
        ],
        axis=axis_pos,
    )
    above = jnp.concatenate(
        [lax.slice_in_dim(cube_vals, 1, PS, axis=axis_pos), jnp.expand_dims(high_plane, axis_pos)],
        axis=axis_pos,
    )
    return (below, above)


def apply_operator(last_local, kappa_local, held_count, slot_ids):
    channels = last_local.shape[1] + 1
    plane_size = PS * PS
    joined = jnp.concatenate([last_local, kappa_local[:, None]], axis=1)
    cube_vals = joined.reshape(CAP, channels, PS, PS, PS)
    first_face = cube_vals[0, :, 0].reshape(channels, plane_size)
    last_slot = lax.dynamic_index_in_dim(cube_vals, held_count - 1, 0, keepdims=False)
    last_face = last_slot[:, PS - 1].reshape(channels, plane_size)
    x_ghost = extended(jnp.stack([first_face, last_face]), (("px", 0),), 1)
    y_planes = jnp.stack([cube_vals[:, :, :, 0], cube_vals[:, :, :, PS - 1]]).reshape(
        2, CAP, channels, plane_size
    )
    y_ghost = extended(y_planes, (("py", 0),), 1)
    ghost_low = x_ghost[0].reshape(channels, PS, PS)
    ghost_high = x_ghost[3].reshape(channels, PS, PS)
    x_low = jnp.concatenate([ghost_low[None], cube_vals[:-1, :, PS - 1]], axis=0)
    next_faces = jnp.concatenate([cube_vals[1:, :, 0], jnp.zeros_like(cube_vals[:1, :, 0])], axis=0)
    x_high = jnp.where(
        (slot_ids == held_count - 1)[:, None, None, None], ghost_high[None], next_faces
    )
    y_low = y_ghost[0].reshape(CAP, channels, PS, PS)
    y_high = y_ghost[3].reshape(CAP, channels, PS, PS)
    z_zero = jnp.zeros((CAP, channels, PS, PS), jnp.float32)
    centre_vals = cube_vals[:, :-1]
    centre_kappa = cube_vals[:, -1:]
    diag_sum = jnp.zeros_like(centre_kappa)
    weighted = jnp.zeros_like(centre_vals)
    for low_plane, high_plane, axis_pos in (
        (x_low, x_high, 2),
        (y_low, y_high, 3),
        (z_zero, z_zero, 4),
    ):
        kappa_pair = shift_pair(centre_kappa, low_plane[:, -1:], high_plane[:, -1:], axis_pos)
        value_pair = shift_pair(centre_vals, low_plane[:, :-1], high_plane[:, :-1], axis_pos)
        for near_kappa, near_vals in zip(kappa_pair, value_pair):
            weight = 0.5 * (centre_kappa + near_kappa)
            diag_sum = diag_sum + weight
            weighted = weighted + weight * near_vals
    summed = diag_sum * centre_vals - weighted
    return summed.reshape(CAP, channels - 1, CELLS)


def normal_parts(sketch_cols, proj_coef, previous_coef, residual_factor):
    pair_count = proj_coef.shape[0]
    width_rhs = proj_coef.shape[1]
    pair_rows = sketch_cols[:pair_count]
    first_image = jnp.einsum("ab,ak->bk", previous_coef, pair_rows, precision=highest)
    second_image = (
        jnp.einsum("ab,ak->bk", proj_coef, pair_rows, precision=highest) + sketch_cols[pair_count:]
    )
    images = jnp.concatenate([first_image, second_image], axis=0)
    target = jnp.einsum("ab,ak->bk", residual_factor, sketch_cols[:width_rhs], precision=highest)
    return (
        jnp.dot(images, images.T, precision=highest),
        jnp.dot(images, target.T, precision=highest),
    )


def solve_normal(normal_gram, normal_cross):
    factor_low = jnp.linalg.cholesky(normal_gram)
    middle = lax.linalg.triangular_solve(factor_low, normal_cross, left_side=True, lower=True)
    return lax.linalg.triangular_solve(
        factor_low, middle, left_side=True, lower=True, transpose_a=True
    )


def body(
    counts, coefficient, signs, basis_old, basis_last, residual_factor, previous_coef, sample_rows
):
    px_index = lax.axis_index("px")
    py_index = lax.axis_index("py")
    py_count = lax.axis_size("py")
    device_count = lax.axis_size("px") * py_count
    total_cells = MEANX * device_count * CELLS
    offsets = jnp.cumsum(counts) - counts
    held_count = counts[px_index]
    slot_ids = jnp.arange(CAP, dtype=jnp.int32)
    live_weight = (slot_ids < held_count).astype(jnp.float32)
    old_local = basis_old[:, 0] * live_weight[:, None, None]
    last_local = basis_last[:, 0] * live_weight[:, None, None]
    image = (
        apply_operator(last_local, coefficient[:, 0], held_count, slot_ids)
        * live_weight[:, None, None]
    )
    pair = jnp.concatenate([old_local, last_local], axis=1)
    local_gram = jnp.einsum("sac,sbc->ab", pair, image, precision=highest)
    patch_ids = (offsets[px_index] + slot_ids) * py_count + py_index
    sign_flips = (1 - 2 * signs[:, 0]).astype(jnp.float32)
    share_width = K // device_count
    share_start = (px_index * py_count + py_index) * share_width
    proj_coef = lax.psum(local_gram, ("px", "py")) / total_cells
    new_local = image - jnp.einsum("sac,ab->sbc", pair, proj_coef, precision=highest)
    spread = transform_cells(jnp.concatenate([pair, new_local], axis=1) * sign_flips[:, None, :])
    picked = jnp.take(spread, sample_rows % CELLS, axis=2)
    parity = parity_of(jnp.bitwise_and(patch_ids[:, None], (sample_rows // CELLS)[None, :]))
    weights = (1 - 2 * parity).astype(jnp.float32) * live_weight[:, None]
    partial_value = jnp.einsum("sk,sjk->jk", weights, picked, precision=highest) * (
        1.0 / math.sqrt(total_cells)
    )
    sketch_whole = lax.psum(partial_value, ("px", "py"))
    sketch_mine = lax.dynamic_slice_in_dim(sketch_whole, share_start, share_width, 1)
    normal_gram, normal_cross = normal_parts(
        sketch_whole, proj_coef, previous_coef, residual_factor
    )
    solution = solve_normal(normal_gram, normal_cross)
    return (new_local[:, None], sketch_mine, solution)


def solution(mesh):
    in_specs = (
        P(),
        P("px", "py", None),
        P("px", "py", None),
        P("px", "py", None, None),
        P("px", "py", None, None),
        P(),
        P(),
        P(),
    )
    out_specs = (P("px", "py", None, None), P(None, ("px", "py")), P())
    return jax.shard_map(body, mesh=mesh, in_specs=in_specs, out_specs=out_specs, check_vma=False)
```

profile of v0, /device:TPU:0, one launch (start us, length us, event | category | flops | bytes accessed | tf_op | source)
XLA Modules:
  0.0 452.1 jit_solution(10791391450854950705)
XLA Ops:
  7.2 1.2 dynamic_slice.13
  9.1 2.3 bitcast_multiply_fusion.2
  11.7 2.3 copy.19
  14.0 8.6 %reshape.92 = f32[6,17,16,16,16]{4,3,2,0,1:T(8,128)} reshape(f32[6,17,4096]{2,0,1:T(8,128)} %copy.19) | data formatting | bytes 3342336 | tf_op jit(solution)/shard_map/reshape | solution.py:72
  23.6 1.3 collective-permute-start.1
  26.2 3.2 constant_dynamic-slice_fusion.1
  29.4 3.9 copy.20
  34.3 6.1 %collective-permute-start = (f32[1,17,256]{2,0,1:T(1,128)S(1)}, f32[1,17,256]{2,0,1:T(1,128)}, u32[]{:S(2)}, u32[]{:S(2)}) collective-permute-start(f32[1,17,256]{2,0,1:T(1,128)S(1)} %copy.42), channel_id=1, source_target_pairs={{0,4},{4,8},{8,12},{12,16},{16,20},{20,24},{24,28},{1,5},{5,9},{9,... | collective-permute-start | bytes 52232 | tf_op jit(solution)/shard_map/ppermute | solution.py:23
  40.3 10.8 %slice_reduce_fusion = (f32[6,17,16,16]{3,2,0,1:T(8,128)}, f32[6,17,16,16]{3,2,0,1:T(8,128)}) fusion(f32[6,17,16,16,16]{4,3,2,0,1:T(8,128)} %reshape.92), kind=kLoop, calls=%fused_computation.34 | loop fusion | bytes 417792 | tf_op jit(solution)/shard_map/slice | solution.py:77
  51.1 1.5 reshape.112
  53.4 2.1 collective-permute-start.2
  55.5 1.5 reshape.113
  57.7 1.8 collective-permute-start.3
  59.5 18.2 %fusion.102 = (f32[6,16,15,16,16]{4,3,2,0,1:T(8,128)}, f32[6,16,15,16,16]{4,3,2,0,1:T(8,128)}) fusion(f32[6,17,16,16,16]{4,3,2,0,1:T(8,128)} %reshape.92), kind=kLoop, calls=%fused_computation.174 | loop fusion | bytes 5898240 | tf_op jit(solution)/shard_map/slice | solution.py:62
  77.8 1.2 slice_bitcast_fusion.1
  79.0 9.1 %fusion.101 = (f32[6,16,16,15,16]{4,3,2,0,1:T(8,128)}, f32[6,16,16,15,16]{4,3,2,0,1:T(8,128)}) fusion(f32[6,17,16,16,16]{4,3,2,0,1:T(8,128)S(1)} %bitcast.141), kind=kLoop, calls=%fused_computation.173 | loop fusion | bytes 5898240 | tf_op jit(solution)/shard_map/slice | solution.py:62
  88.1 9.8 %fusion.100 = (f32[6,16,16,16,15]{4,3,2,0,1:T(8,128)}, f32[6,16,16,16,15]{4,3,2,0,1:T(8,128)}) fusion(f32[6,17,16,16,16]{4,3,2,0,1:T(8,128)S(1)} %bitcast.141), kind=kLoop, calls=%fused_computation.172 | loop fusion | bytes 5898240 | tf_op jit(solution)/shard_map/slice | solution.py:57
  97.9 1.4 fusion.99
  99.3 1.3 fusion.97
  100.6 1.3 fusion.98
  103.1 1.4 copy.50
  104.5 1.4 copy.51
  106.8 4.0 bitcast_multiply_fusion.1
  112.1 1.3 copy.49
  114.5 1.3 pad_select_fusion
  116.7 3.5 fusion.30
  120.2 1.3 slice_bitcast_fusion
  123.6 2.1 slice.185
  125.7 1.4 slice.175
  129.2 2.1 slice.182
  132.1 5.0 %add_bitcast_fusion = (f32[6,16,16,16]{3,2,1,0:T(8,128)}, f32[6,16,16,16]{3,2,1,0:T(8,128)}, f32[6,16,16,16]{3,2,1,0:T(8,128)}, f32[6,16,16,16]{3,2,1,0:T(8,128)}) fusion(f32[6,1,16,16,15]{4,3,2,0,1:T(8,128)} %get-tuple-element.22, f32[6,17,16,16,16]{4,3,2,0,1:T(8,128)} %reshape.92, f32[6,1,16,16,15]{4,3,2,0,1:T(8,128)} %get-tuple-element.23, ...), kind=kLoop, calls=%fused_computation.48 | loop fusion | flops 516096 | bytes 1069056 | tf_op jit(solution)/shard_map/mul | solution.py:106
  137.1 37.8 %fusion = f32[6,16,16,16,16]{4,3,2,0,1:T(8,128)} fusion(f32[6,17,16,16,16]{4,3,2,0,1:T(8,128)} %reshape.92, f32[6,16,15,16,16]{4,3,2,0,1:T(8,128)} %get-tuple-element.29, f32[6,16,1,16,16]{4,3,2,0,1:T(8,128)} %get-tuple-element.41, f32[6,16,1,16,16]{4,3,2,0,1:T(8,128)} %get-tuple-element.40, f32[6,16,15,16,16]{4,3,2,0,1:T(8,128)} %get-tuple-element.28, ...), kind=kLoop, calls=%fused_computation.2 | loop fusion | flops 6684672 | bytes 13074432 | tf_op jit(solution)/shard_map/sub | solution.py:106
  174.9 10.5 %reshape.114 = f32[6,16,4096]{2,0,1:T(8,128)} reshape(f32[6,16,16,16,16]{4,3,2,0,1:T(8,128)} %fusion) | data formatting | bytes 3145728 | tf_op jit(solution)/shard_map/reshape | solution.py:107
  185.4 4.7 %fusion.14 = f32[32,16]{0,1:T(8,128)S(1)} fusion(f32[6,16,4096]{2,0,1:T(8,128)} %reshape.114, f32[6,16,4096]{2,1,0:T(8,128)S(1)} %get-tuple-element.37, f32[6,16,4096]{2,1,0:T(8,128)S(1)} %get-tuple-element.36, f32[6]{0:T(128)S(1)} %copy-done.13), kind=kOutput, calls=%fused_computation.33 | convolution fusion | flops 152174592 | bytes 4720664 | tf_op jit(solution)/shard_map/sac,sbc->ab/dot_general | solution.py:153
  190.2 51.3 %psum.14 = f32[32,16]{0,1:T(8,128)S(1)} all-reduce(f32[32,16]{0,1:T(8,128)S(1)} %fusion.14), channel_id=1, replica_groups=mesh['px'=8,'py'=4] {'px','py'}, use_global_device_ids=true, to_apply=%region_0.0 | all-reduce | flops 512 | bytes 4096 | tf_op jit(solution)/shard_map/psum | solution.py:158
  241.5 4.1 fusion.6
  246.8 4.0 fusion.7
  250.8 5.7 %convolution_bitcast_fusion.1 = f32[6,48,32,128]{3,2,1,0:T(8,128)} fusion(f32[6,48,32,128]{3,2,1,0:T(8,128)S(1)} %fusion.7), kind=kOutput, calls=%fused_computation.25 | convolution fusion | flops 453000192 | bytes 9437184 | tf_op jit(solution)/shard_map/ca,sjad->sjcd/dot_general | solution.py:49
  256.5 9.7 %copy.46 = f32[6,48,32,128]{1,0,3,2:T(8,128)} copy(f32[6,48,32,128]{3,2,1,0:T(8,128)} %convolution_bitcast_fusion.1) | data formatting | bytes 9437184 | tf_op jit(solution)/shard_map/reshape | solution.py:50
  266.1 21.7 %gather_fusion = f32[2048,6,48]{2,1,0:T(8,128)} fusion(f32[6,48,4096]{1,0,2:T(8,128)} %bitcast.142, s32[2048]{0:T(1024)S(1)} %copy-done.10), kind=kCustom, calls=%fused_computation | custom fusion | bytes 4726784 | tf_op jit(solution)/shard_map/jit(_take)/gather | solution.py:161
  287.8 13.2 %multiply_reduce_fusion = f32[2048,48]{1,0:T(8,128)S(1)} fusion(f32[2048,6,48]{2,1,0:T(8,128)} %gather_fusion, f32[2048,6]{1,0:T(8,128)S(1)} %copy-done.7, pred[2048]{0:T(1024)(128)(4,1)S(1)} %copy-done.15), kind=kLoop, calls=%fused_computation.12 | loop fusion | flops 1671168 | bytes 2803712
  302.2 127.4 %all-reduce.7.cloned.1.call-done = f32[48,2048]{1,0:T(8,128)} async-done(((f32[48,2048]{1,0:T(8,128)}), f32[48,2048]{1,0:T(8,128)}) %all-reduce.7.cloned.1.call-update) | async-done | bytes 393232 | tf_op jit(solution)/shard_map/psum | solution.py:167
  429.5 1.2 convolution_add_fusion
  430.8 1.2 convolution_bitcast_fusion.2
  432.4 2.7 fusion.27
  435.9 2.9 cholesky.16
  440.1 2.4 custom-call.8
  443.6 1.4 constant_dynamic-slice_fusion
  (88 shorter events, 20.4 us)
Async XLA Ops:
  7.2 423.6 %copy-start = (f32[32,16]{0,1:T(8,128)S(1)}, f32[32,16]{0,1:T(8,128)}, u32[]{:S(2)}) copy-start(f32[32,16]{0,1:T(8,128)} %param.14) | copy-start | bytes 6148
  7.2 4.3 copy-start.9
  7.2 422.3 %all-reduce.7.cloned.1.call-start = ((), (), s32[]{:S(2)}) async-start(), calls=%async_computation | async-start | bytes 786432 | tf_op jit(solution)/shard_map/psum | solution.py:167
  9.1 102.3 %copy-start.12 = (f32[6]{0:T(128)}, f32[6]{0:T(128)S(1)}, u32[]{:S(2)}) copy-start(f32[6]{0:T(128)S(1)} %compare_convert_fusion) | copy-start | bytes 76
  23.6 89.8 %collective-permute-start.1 = (f32[1,17,256]{2,0,1:T(1,128)S(1)}, f32[1,17,256]{2,0,1:T(1,128)S(1)}, u32[]{:S(2)}, u32[]{:S(2)}) collective-permute-start(f32[1,17,256]{2,0,1:T(1,128)S(1)} %stack_reshape_squeeze.7), channel_id=1, source_target_pairs={{4,0},{8,4},{12,8},{16,12},{20,16},{24,20},{28,24},{5,1},{9,5},{13... | collective-permute-start | bytes 52232 | tf_op jit(solution)/shard_map/ppermute | solution.py:26
  34.3 79.4 %collective-permute-start = (f32[1,17,256]{2,0,1:T(1,128)S(1)}, f32[1,17,256]{2,0,1:T(1,128)}, u32[]{:S(2)}, u32[]{:S(2)}) collective-permute-start(f32[1,17,256]{2,0,1:T(1,128)S(1)} %copy.42), channel_id=1, source_target_pairs={{0,4},{4,8},{8,12},{12,16},{16,20},{20,24},{24,28},{1,5},{5,9},{9,... | collective-permute-start | bytes 52232 | tf_op jit(solution)/shard_map/ppermute | solution.py:23
  53.4 73.8 %collective-permute-start.2 = (f32[1,6,17,256]{3,0,2,1:T(1,128)}, f32[1,6,17,256]{3,0,2,1:T(1,128)}, u32[]{:S(2)}, u32[]{:S(2)}) collective-permute-start(f32[1,6,17,256]{3,0,2,1:T(1,128)} %copy.43), channel_id=1, source_target_pairs={{0,1},{1,2},{2,3},{4,5},{5,6},{6,7},{8,9},{9,10},{10,11},{12,13},{... | collective-permute-start | bytes 313352 | tf_op jit(solution)/shard_map/ppermute | solution.py:23
  57.0 20.8 %slice-start = ((s8[13369344]{0:T(1024)(128)(4,1)}), s8[4194304]{0:T(1024)(128)(4,1)S(1)}, s32[]{:S(2)}) async-start(s8[13369344]{0:T(1024)(128)(4,1)} %bitcast.140), calls=%async_computation.1 | async-start | bytes 8388608
  57.7 20.1 %slice-start.1 = ((s8[13369344]{0:T(1024)(128)(4,1)}), s8[4194304]{0:T(1024)(128)(4,1)S(1)}, s32[]{:S(2)}) async-start(s8[13369344]{0:T(1024)(128)(4,1)} %bitcast.140), calls=%async_computation.2 | async-start | bytes 8388608
  57.7 20.1 %slice-start.2 = ((s8[13369344]{0:T(1024)(128)(4,1)}), s8[4194304]{0:T(1024)(128)(4,1)S(1)}, s32[]{:S(2)}) async-start(s8[13369344]{0:T(1024)(128)(4,1)} %bitcast.140), calls=%async_computation.3 | async-start | bytes 8388608
  57.7 20.1 %slice-start.3 = ((s8[13369344]{0:T(1024)(128)(4,1)}), s8[786432]{0:T(1024)(128)(4,1)S(1)}, s32[]{:S(2)}) async-start(s8[13369344]{0:T(1024)(128)(4,1)} %bitcast.140), calls=%async_computation.4 | async-start | bytes 1572864
  57.7 63.8 %collective-permute-start.3 = (f32[1,6,17,256]{3,0,2,1:T(1,128)}, f32[1,6,17,256]{3,0,2,1:T(1,128)}, u32[]{:S(2)}, u32[]{:S(2)}) collective-permute-start(f32[1,6,17,256]{3,0,2,1:T(1,128)} %copy.44), channel_id=1, source_target_pairs={{1,0},{2,1},{3,2},{5,4},{6,5},{7,6},{9,8},{10,9},{11,10},{13,12},{... | collective-permute-start | bytes 313352 | tf_op jit(solution)/shard_map/ppermute | solution.py:26
  97.9 4.0 copy-start.11
  97.9 5.2 %copy-start.3 = (f32[6,1,16,4096]{3,2,1,0:T(8,128)S(1)}, f32[6,1,16,4096]{3,2,1,0:T(8,128)}, u32[]{:S(2)}) copy-start(f32[6,1,16,4096]{3,2,1,0:T(8,128)} %param.11) | copy-start | bytes 4718596
  99.3 5.2 %copy-start.4 = (f32[6,1,16,4096]{3,2,1,0:T(8,128)S(1)}, f32[6,1,16,4096]{3,2,1,0:T(8,128)}, u32[]{:S(2)}) copy-start(f32[6,1,16,4096]{3,2,1,0:T(8,128)} %param.12) | copy-start | bytes 4718596
  100.6 5.4 %copy-start.8 = (s32[6,1,4096]{2,1,0:T(1,128)S(1)}, s32[6,1,4096]{2,1,0:T(1,128)}, u32[]{:S(2)}) copy-start(s32[6,1,4096]{2,1,0:T(1,128)} %param.10) | copy-start | bytes 294916
  100.6 5.5 %copy-start.16 = (s32[8]{0:T(128)S(1)}, s32[8]{0:T(128)}, u32[]{:S(2)}) copy-start(s32[8]{0:T(128)} %param.8) | copy-start | bytes 100
  114.5 5.6 %copy-start.6 = (f32[5,17,16,16]{3,2,0,1:T(8,128)S(1)}, f32[5,17,16,16]{3,2,0,1:T(8,128)}, u32[]{:S(2)}) copy-start(f32[5,17,16,16]{3,2,0,1:T(8,128)} %get-tuple-element.31) | copy-start | bytes 261124
  174.9 10.5 %copy-start.13 = (f32[6]{0:T(128)S(1)}, f32[6]{0:T(128)}, u32[]{:S(2)}) copy-start(f32[6]{0:T(128)} %copy-done.12) | copy-start | bytes 76
  241.5 5.3 %copy-start.1 = (f32[6,16,32,128]{3,2,1,0:T(8,128)S(1)}, f32[6,16,32,128]{3,2,1,0:T(8,128)}, u32[]{:S(2)}) copy-start(f32[6,16,32,128]{3,2,1,0:T(8,128)} %get-tuple-element.34) | copy-start | bytes 4718596
  241.5 5.3 %copy-start.2 = (f32[6,16,32,128]{3,2,1,0:T(8,128)S(1)}, f32[6,16,32,128]{3,2,1,0:T(8,128)}, u32[]{:S(2)}) copy-start(f32[6,16,32,128]{3,2,1,0:T(8,128)} %get-tuple-element.35) | copy-start | bytes 4718596
  245.6 1.1 copy-start.5
  256.5 9.7 %copy-start.10 = (s32[2048]{0:T(1024)S(1)}, s32[2048]{0:T(1024)}, u32[]{:S(2)}) copy-start(s32[2048]{0:T(1024)} %get-tuple-element.33) | copy-start | bytes 24580
  266.1 21.7 %copy-start.7 = (f32[2048,6]{1,0:T(8,128)S(1)}, f32[2048,6]{1,0:T(8,128)}, u32[]{:S(2)}) copy-start(f32[2048,6]{1,0:T(8,128)} %copy.49) | copy-start | bytes 147460
  266.1 21.7 %copy-start.15 = (pred[2048]{0:T(1024)(128)(4,1)S(1)}, pred[2048]{0:T(1024)(128)(4,1)}, u32[]{:S(2)}) copy-start(pred[2048]{0:T(1024)(128)(4,1)} %compare_and_fusion) | copy-start | bytes 6148
  287.8 144.6 %copy-start.14 = (f32[16,16]{1,0:T(8,128)S(1)}, f32[16,16]{1,0:T(8,128)}, u32[]{:S(2)}) copy-start(f32[16,16]{1,0:T(8,128)} %param.13) | copy-start | bytes 3076
Sparse Core Ops, SparseCore 0:
  302.3 127.2 all-reduce.6
where the time goes:
time: 456 us; the launch traced here: 452 us
  local copies, waits for them, and re-layouts  139 us (30%)
  waiting for transfers between devices  127 us (28%)
  other arithmetic  81.1 us (18%)
  blocking collectives  51.3 us (11%)
  matrix products  25.8 us (6%)
  between operations  15.9 us (3%)
  starting transfers between devices  11.3 us (2%)
    psum x1, waiting for transfers between devices, body(): sketch_whole = lax.psum(partial_value, ('px', 'py'))  127 us
    psum x1, blocking collectives, body(): proj_coef = lax.psum(local_gram, ('px', 'py')) / total_cells  51.3 us
    sub x1, other arithmetic, apply_operator(): summed = diag_sum * centre_vals - weighted  37.8 us
    slice x2, local copies, waits for them, and re-layouts, shift_pair(): lax.slice_in_dim(cube_vals, 1, PS, axis=axis_pos)  27.3 us
    gather x1, local copies, waits for them, and re-layouts, body(): picked = jnp.take(spread, sample_rows % CELLS, axis=2)  21.7 us
    slice x4, local copies, waits for them, and re-layouts, shift_pair(): lax.slice_in_dim(cube_vals, 0, PS - 1, axis=axis_pos)  13.8 us
    unnamed x3, other arithmetic  13.3 us
    slice x1, local copies, waits for them, and re-layouts, apply_operator(): cube_vals[:, :, :, 0]  10.8 us
  transfers between devices with their start and end apart: 5, of which 1 were waited for; matrix products, arithmetic and copies ran while one was open for 20% of the time, Pallas kernels for 0%

commit v1 on v0

v1 whole, which is shorter than its diff:
```python
import functools
import math

import jax
import jax.numpy as jnp
from jax import lax
from jax.experimental import pallas as pl
from jax.experimental.pallas import tpu as pltpu
from jax.sharding import PartitionSpec as P

PS = 16
MEANX = 2
TILE = 256

highest = lax.Precision.HIGHEST
f32 = jnp.float32
bf16 = jnp.bfloat16
VMEM = pl.BlockSpec(memory_space=pltpu.VMEM)
SMEM = pl.BlockSpec(memory_space=pltpu.SMEM)


def params(**more):
    return pltpu.CompilerParams(vmem_limit_bytes=48 * 1024 * 1024, **more)


def parity_sign(values, bits):
    amount = 1
    while amount < bits:
        amount *= 2
    while amount > 1:
        amount //= 2
        values = jnp.bitwise_xor(values, jnp.right_shift(values, amount))
    return 1 - 2 * jnp.bitwise_and(values, 1)


def halo_kernel(
    n_px, n_py, counts_ref, last_ref, kap_ref, yg_ref, xg_ref, ybuf, xbuf, ysend, yrecv, xsend, xrecv
):
    i = lax.axis_index("px")
    j = lax.axis_index("py")
    cap = last_ref.shape[0]
    rhs = last_ref.shape[2]
    plane = PS * PS
    barrier = pltpu.get_barrier_semaphore()
    around = [
        ("py", j - 1, j > 0),
        ("py", j + 1, j < n_py - 1),
        ("px", i - 1, i > 0),
        ("px", i + 1, i < n_px - 1),
    ]
    for axis, index, valid in around:
        @pl.when(valid)
        def _(axis=axis, index=index):
            pl.semaphore_signal(
                barrier, inc=1, device_id={axis: index}, device_id_type=pl.DeviceIdType.MESH
            )

    lane = lax.broadcasted_iota(jnp.int32, (1, plane), 1)
    tail = jnp.clip(counts_ref[i] - 1, 0, cap - 1)
    xbuf[0, pl.ds(0, rhs), :] = last_ref[0, 0, :, pl.ds(0, plane)]
    xbuf[0, pl.ds(rhs, 1), :] = kap_ref[0, :, pl.ds(0, plane)]
    top = (PS - 1) * plane
    xbuf[1, pl.ds(0, rhs), :] = last_ref[tail, 0, :, pl.ds(top, plane)]
    xbuf[1, pl.ds(rhs, 1), :] = kap_ref[tail, :, pl.ds(top, plane)]

    def pack(s, carry):
        u0 = jnp.zeros((rhs, plane), f32)
        u1 = jnp.zeros((rhs, plane), f32)
        k0 = jnp.zeros((1, plane), f32)
        k1 = jnp.zeros((1, plane), f32)
        for a in range(PS):
            mine = lane // PS == a
            u = last_ref[s, 0, :, pl.ds(a * plane, plane)]
            k = kap_ref[s, :, pl.ds(a * plane, plane)]
            lo = (a * PS) % plane
            hi = (a * PS + PS) % plane
            u0 = jnp.where(mine, pltpu.roll(u, lo, 1) if lo else u, u0)
            u1 = jnp.where(mine, pltpu.roll(u, hi, 1) if hi else u, u1)
            k0 = jnp.where(mine, pltpu.roll(k, lo, 1) if lo else k, k0)
            k1 = jnp.where(mine, pltpu.roll(k, hi, 1) if hi else k, k1)
        ybuf[0, pl.ds(pl.multiple_of(s * rhs, 8), rhs), :] = u0
        ybuf[1, pl.ds(pl.multiple_of(s * rhs, 8), rhs), :] = u1
        ybuf[0, pl.ds(cap * rhs + s, 1), :] = k0
        ybuf[1, pl.ds(cap * rhs + s, 1), :] = k1
        return carry

    peers = sum(valid.astype(jnp.int32) for _, _, valid in around)
    pl.semaphore_wait(barrier, peers)

    def copy_of(base, side):
        axis, index, _ = around[base + side]
        buf, ghost, send, recv = (
            (xbuf, xg_ref, xsend, xrecv) if base == 2 else (ybuf, yg_ref, ysend, yrecv)
        )
        return pltpu.make_async_remote_copy(
            src_ref=buf.at[side],
            dst_ref=ghost.at[1 - side],
            send_sem=send.at[side],
            recv_sem=recv.at[1 - side],
            device_id={axis: index},
            device_id_type=pl.DeviceIdType.MESH,
        )

    for side in range(2):
        @pl.when(around[2 + side][2])
        def _(side=side):
            copy_of(2, side).start()

    lax.fori_loop(0, cap, pack, 0)

    for side in range(2):
        @pl.when(around[side][2])
        def _(side=side):
            copy_of(0, side).start()
    for base, ghost in ((0, yg_ref), (2, xg_ref)):
        for side in range(2):
            @pl.when(jnp.logical_not(around[base + side][2]))
            def _(ghost=ghost, side=side):
                ghost[side] = jnp.zeros(ghost.shape[1:], f32)
    for base in (2, 0):
        for side in range(2):
            @pl.when(around[base + side][2])
            def _(base=base, side=side):
                copy_of(base, side).wait_send()
    for base, ghost, buf, send, recv in (
        (2, xg_ref, xbuf, xsend, xrecv),
        (0, yg_ref, ybuf, ysend, yrecv),
    ):
        for side in range(2):
            axis, index, valid = around[base + side]

            @pl.when(valid)
            def _(ghost=ghost, buf=buf, side=side, send=send, recv=recv, axis=axis, index=index):
                pltpu.make_async_remote_copy(
                    src_ref=buf.at[side],
                    dst_ref=ghost.at[side],
                    send_sem=send.at[side],
                    recv_sem=recv.at[side],
                    device_id={axis: index},
                    device_id_type=pl.DeviceIdType.MESH,
                ).wait_recv()


def halo(n_px, n_py, counts, last, kap):
    cap, _, rhs, _ = last.shape
    plane = PS * PS
    yrows = cap * rhs + -(-cap // 8) * 8
    xrows = rhs + 8
    return pl.pallas_call(
        functools.partial(halo_kernel, n_px, n_py),
        out_shape=(
            jax.ShapeDtypeStruct((2, yrows, plane), f32),
            jax.ShapeDtypeStruct((2, xrows, plane), f32),
        ),
        in_specs=[SMEM, VMEM, VMEM],
        out_specs=(VMEM, VMEM),
        scratch_shapes=[
            pltpu.VMEM((2, yrows, plane), f32),
            pltpu.VMEM((2, xrows, plane), f32),
            pltpu.SemaphoreType.DMA((2,)),
            pltpu.SemaphoreType.DMA((2,)),
            pltpu.SemaphoreType.DMA((2,)),
            pltpu.SemaphoreType.DMA((2,)),
        ],
        compiler_params=params(collective_id=0, has_side_effects=True),
    )(counts, last, kap)


def split(values):
    head = values.astype(bf16)
    return head, (values - head.astype(f32)).astype(bf16)


def local_kernel(
    n_py, scale, counts_ref, last_ref, old_ref, kap_ref, sgn_ref, yg_ref, xg_ref, rows_ref,
    image_ref, gram_ref, sketch_ref, cols, table,
):
    i = lax.axis_index("px")
    j = lax.axis_index("py")
    cap, _, rhs, cells = last_ref.shape
    plane = PS * PS
    held = counts_ref[i]
    offset = lax.fori_loop(0, i, lambda t, acc: acc + counts_ref[t], jnp.int32(0))
    lane = lax.broadcasted_iota(jnp.int32, (1, plane), 1)
    b_id = lane // PS
    c_id = lane % PS
    top = (PS - 1) * plane

    def one_slot(s, carry):
        live = s < held
        first = s == 0
        final = s == held - 1
        before = jnp.maximum(s - 1, 0)
        after = jnp.minimum(s + 1, cap - 1)
        ks = pl.ds(cap * rhs + s, 1)
        us = pl.ds(pl.multiple_of(s * rhs, 8), rhs)
        kg_lo, kg_hi = yg_ref[0, ks, :], yg_ref[1, ks, :]
        ug_lo, ug_hi = yg_ref[0, us, :], yg_ref[1, us, :]
        for a in range(PS):
            at = pl.ds(a * plane, plane)

            def planes(ref_at, ghost_rows):
                if a == 0:
                    low = jnp.where(first, xg_ref[0, ghost_rows, :], ref_at(before, top))
                else:
                    low = ref_at(s, (a - 1) * plane)
                if a == PS - 1:
                    high = jnp.where(final, xg_ref[1, ghost_rows, :], ref_at(after, 0))
                else:
                    high = ref_at(s, (a + 1) * plane)
                return low, high

            def rolled(value, glo, ghi):
                lo = (plane - a * PS) % plane
                hi = (plane - PS - a * PS) % plane
                blo = jnp.where(
                    b_id == 0, pltpu.roll(glo, lo, 1) if lo else glo, pltpu.roll(value, PS, 1)
                )
                bhi = jnp.where(
                    b_id == PS - 1,
                    pltpu.roll(ghi, hi, 1) if hi else ghi,
                    pltpu.roll(value, plane - PS, 1),
                )
                return blo, bhi, pltpu.roll(value, 1, 1), pltpu.roll(value, plane - 1, 1)

            k = kap_ref[s, :, at]
            u = last_ref[s, 0, :, at]
            ka = planes(lambda t, p: kap_ref[t, :, pl.ds(p, plane)], pl.ds(rhs, 1))
            ua = planes(lambda t, p: last_ref[t, 0, :, pl.ds(p, plane)], pl.ds(0, rhs))
            kr = rolled(k, kg_lo, kg_hi)
            ur = rolled(u, ug_lo, ug_hi)
            kc = (jnp.where(c_id == 0, 0.0, kr[2]), jnp.where(c_id == PS - 1, 0.0, kr[3]))
            near_k = (ka[0], ka[1], kr[0], kr[1], kc[0], kc[1])
            near_u = (ua[0], ua[1]) + ur
            weights = [0.5 * (k + kn) for kn in near_k]
            diag = weights[0]
            for w in weights[1:]:
                diag = diag + w
            weights[4] = jnp.where(c_id == 0, 0.0, weights[4])
            weights[5] = jnp.where(c_id == PS - 1, 0.0, weights[5])
            image = diag * u
            for w, un in zip(weights, near_u):
                image = image - w * un
            image = jnp.where(live, image, 0.0)
            image_ref[s, :, at] = image
            sg = jnp.where(live, 1 - 2 * sgn_ref[s, :, at], 0).astype(f32)
            for part, value in enumerate((old_ref[s, 0, :, at], u, image)):
                head, tail = split(value * sg)
                cols[s, pl.ds(part * rhs, rhs), at] = head
                cols[s, pl.ds((part + 3) * rhs, rhs), at] = tail
        return carry

    lax.fori_loop(0, cap, one_slot, 0)

    def one_gram(s, acc):
        whole = cols[s]
        imgs = jnp.concatenate(
            [whole[2 * rhs:3 * rhs], whole[5 * rhs:6 * rhs]], axis=0
        )
        both = lax.dot_general(
            whole, imgs, (((1,), (1,)), ((), ())), preferred_element_type=f32
        )
        both = both[:2 * rhs] + both[3 * rhs:5 * rhs]
        return acc + both[:, :rhs] + both[:, rhs:]

    gram_ref[...] = lax.fori_loop(0, cap, one_gram, jnp.zeros((2 * rhs, rhs), f32))

    cell_bits = cells.bit_length() - 1
    inner = lax.broadcasted_iota(jnp.int32, (TILE, TILE), 0)
    outer = cells // TILE
    hi_ids = lax.broadcasted_iota(jnp.int32, (outer, TILE), 0)

    def one_tile(t, carry):
        at = pl.ds(pl.multiple_of(t * TILE, TILE), TILE)
        rows = rows_ref[:, at]
        inside = parity_sign(jnp.bitwise_and(inner, rows), 8).astype(f32).astype(bf16)
        across = parity_sign(
            jnp.bitwise_and(hi_ids, jnp.right_shift(rows, 8) & (outer - 1)), 4
        ).astype(f32)
        for h in range(outer):
            table[pl.ds(h * TILE, TILE), :] = inside * across[h:h + 1].astype(bf16)
        flat = cols[...].reshape(cap * 6 * rhs, cells)
        spread = jnp.dot(flat, table[...], preferred_element_type=f32)
        total = jnp.zeros((3 * rhs, TILE), f32)
        for s in range(cap):
            patch = (offset + s) * n_py + j
            w = parity_sign(
                jnp.bitwise_and(jnp.right_shift(rows, cell_bits), patch), 16
            ).astype(f32)
            base = s * 6 * rhs
            total = total + w * (
                spread[base:base + 3 * rhs] + spread[base + 3 * rhs:base + 6 * rhs]
            )
        sketch_ref[:, at] = total * scale
        return carry

    lax.fori_loop(0, rows_ref.shape[1] // TILE, one_tile, 0)


def local_work(n_py, scale, counts, last, old, kap, sgn, yg, xg, rows):
    cap, _, rhs, cells = last.shape
    k = rows.shape[1]
    return pl.pallas_call(
        functools.partial(local_kernel, n_py, scale),
        out_shape=(
            jax.ShapeDtypeStruct((cap, rhs, cells), f32),
            jax.ShapeDtypeStruct((2 * rhs, rhs), f32),
            jax.ShapeDtypeStruct((3 * rhs, k), f32),
        ),
        in_specs=[SMEM] + [VMEM] * 7,
        out_specs=(VMEM, VMEM, VMEM),
        scratch_shapes=[
            pltpu.VMEM((cap, 6 * rhs, cells), bf16),
            pltpu.VMEM((cells, TILE), bf16),
        ],
        compiler_params=params(),
    )(counts, last, old, kap, sgn, yg, xg, rows)


def block_kernel(proj_ref, old_ref, last_ref, image_ref, out_ref):
    rhs = old_ref.shape[2]
    proj = proj_ref[...]
    pair = jnp.concatenate([old_ref[0, 0], last_ref[0, 0]], axis=0)
    moved = lax.dot_general(
        proj, pair, (((0,), (0,)), ((), ())), precision=highest, preferred_element_type=f32
    )
    out_ref[0, 0] = image_ref[0] - moved


def masked_block_kernel(counts_ref, proj_ref, old_ref, last_ref, image_ref, out_ref):
    s = pl.program_id(0)
    held = counts_ref[lax.axis_index("px")]

    @pl.when(s < held)
    def _():
        block_kernel(proj_ref, old_ref, last_ref, image_ref, out_ref)

    @pl.when(s >= held)
    def _():
        out_ref[...] = jnp.zeros(out_ref.shape, f32)


def new_block_of(counts, proj, old, last, image):
    cap, _, rhs, cells = last.shape
    wide = pl.BlockSpec((1, 1, rhs, cells), lambda s: (s, 0, 0, 0))
    return pl.pallas_call(
        masked_block_kernel,
        grid=(cap,),
        out_shape=jax.ShapeDtypeStruct(last.shape, f32),
        in_specs=[
            SMEM,
            pl.BlockSpec(proj.shape, lambda s: (0, 0)),
            wide,
            wide,
            pl.BlockSpec((1, rhs, cells), lambda s: (s, 0, 0)),
        ],
        out_specs=wide,
        compiler_params=params(),
    )(counts, proj, old, last, image)


def tn(left, right):
    return lax.dot_general(
        left, right, (((0,), (0,)), ((), ())), precision=highest, preferred_element_type=f32
    )


def nt(left, right):
    return lax.dot_general(
        left, right, (((1,), (1,)), ((), ())), precision=highest, preferred_element_type=f32
    )


def normal_kernel(rhs, sk_ref, proj_ref, prev_ref, resid_ref, mine_ref, parts_ref):
    pair = sk_ref[pl.ds(0, 2 * rhs), :]
    second = sk_ref[pl.ds(2 * rhs, rhs), :]
    mine_ref[pl.ds(0, 2 * rhs), :] = pair
    mine_ref[pl.ds(2 * rhs, rhs), :] = second - tn(proj_ref[...], pair)
    images = jnp.concatenate([tn(prev_ref[...], pair), second], axis=0)
    target = tn(resid_ref[...], pair[:rhs])
    parts_ref[...] = nt(images, jnp.concatenate([images, target], axis=0))


def normal_parts(sk, proj, prev, resid):
    rhs = resid.shape[0]
    return pl.pallas_call(
        functools.partial(normal_kernel, rhs),
        out_shape=(
            jax.ShapeDtypeStruct(sk.shape, f32),
            jax.ShapeDtypeStruct((2 * rhs, 3 * rhs), f32),
        ),
        compiler_params=params(),
    )(sk, proj, prev, resid)


def eliminate(work):
    size, width = work.shape
    row_id = lax.broadcasted_iota(jnp.int32, (size, 1), 0)
    for step in range(size):
        row = work[step:step + 1, :]
        pivot = row[:, step:step + 1]
        scaled = row / pivot
        column = jnp.where(row_id == step, 0.0, work[:, step:step + 1])
        work = jnp.where(row_id == step, scaled, work - column * scaled)
    return work


def solve_kernel(parts_ref, out_ref):
    size = parts_ref.shape[0]
    out_ref[...] = eliminate(parts_ref[...])[:, size:]


def solve(parts):
    size, width = parts.shape
    return pl.pallas_call(
        solve_kernel,
        out_shape=jax.ShapeDtypeStruct((size, width - size), f32),
        compiler_params=params(),
    )(parts)


def body(
    n_px, n_py, counts, coefficient, signs, basis_old, basis_last, residual_factor, previous_coef,
    sample_rows,
):
    total_cells = MEANX * n_px * n_py * coefficient.shape[2]
    rows = sample_rows.reshape(1, -1)
    yg, xg = halo(n_px, n_py, counts, basis_last, coefficient)
    image, gram, sketch = local_work(
        n_py, 1.0 / math.sqrt(total_cells), counts, basis_last, basis_old, coefficient, signs, yg,
        xg, rows,
    )
    sketch_share = lax.psum_scatter(sketch, ("px", "py"), scatter_dimension=1, tiled=True)
    proj = lax.psum(gram, ("px", "py")) / total_cells
    mine, parts = normal_parts(sketch_share, proj, previous_coef, residual_factor)
    answer = solve(lax.psum(parts, ("px", "py")))
    new_block = new_block_of(counts, proj, basis_old, basis_last, image)
    return (new_block, mine, answer)


def solution(mesh):
    in_specs = (
        P(),
        P("px", "py", None),
        P("px", "py", None),
        P("px", "py", None, None),
        P("px", "py", None, None),
        P(),
        P(),
        P(),
    )
    out_specs = (P("px", "py", None, None), P(None, ("px", "py")), P())
    return jax.shard_map(
        functools.partial(body, mesh.shape["px"], mesh.shape["py"]),
        mesh=mesh,
        in_specs=in_specs,
        out_specs=out_specs,
        check_vma=False,
    )
```

time: 456 us -> 226 us (0.50)
  local copies, waits for them, and re-layouts: 139 us -> 10.5 us
  other arithmetic: 81.1 us -> 0.01 us
  waiting for transfers between devices: 127 us -> 88.3 us
  Pallas kernels: 0 us -> 33.4 us
  blocking collectives: 51.3 us -> 78.2 us
  matrix products: 25.8 us -> 0 us
  starting transfers between devices: 11.3 us -> 0.04 us
    psum x1 -> x0, waiting for transfers between devices: 127 us -> none  [body(): sketch_whole = lax.psum(partial_value, ('px', 'py'))]
    unnamed x1 -> x2, waiting for transfers between devices: 0.02 us -> 88.3 us
    slice x17 -> x0, local copies, waits for them, and re-layouts: 64.6 us -> none  [the longest x2 27.3 us: shift_pair(): lax.slice_in_dim(cube_vals, 1, PS, axis=axis_pos)]
    sub x2 -> x0, other arithmetic: 37.8 us -> none  [the longest x1 37.8 us: apply_operator(): summed = diag_sum * centre_vals - weighted]
    pallas_call x0 -> x5, Pallas kernels: none -> 33.4 us  [the longest x1 18.3 us: local_work(): pl.pallas_call(functools.partial(local_kernel, n_py, scale), out_shape=(j...]
    reshape x3 -> x0, local copies, waits for them, and re-layouts: 28.7 us -> none  [the longest x1 10.5 us: apply_operator(): return summed.reshape(CAP, channels - 1, CELLS)]
    psum x1 -> x2, blocking collectives: 51.3 us -> 78.2 us  [the longest x1 41.3 us: body(): proj = lax.psum(gram, ('px', 'py')) / total_cells]
    dot_general x9 -> x0, matrix products: 24.7 us -> none  [the longest x1 5.68 us: transform_cells(): jnp.einsum('ca,sjad->sjcd', sign_table(outer_len), shaped, precision=high...]
  transfers between devices with their start and end apart: 5 -> 1, of which waited for: 1 -> 1; matrix products, arithmetic and copies ran while one was open for 20% -> 0% of each run, Pallas kernels for 0% -> 2%
where the time goes in v1:
time: 226 us; the launch traced here: 225 us
  waiting for transfers between devices  88.3 us (39%)
  blocking collectives  78.2 us (35%)
  Pallas kernels  33.4 us (15%)
  between operations  14.1 us (6%)
  local copies, waits for them, and re-layouts  10.5 us (5%)
    unnamed x2, waiting for transfers between devices  88.3 us
    psum x1, blocking collectives, body(): proj = lax.psum(gram, ('px', 'py')) / total_cells  41.3 us
    psum x1, blocking collectives, body(): answer = solve(lax.psum(parts, ('px', 'py')))  36.9 us
    pallas_call x1, Pallas kernels, local_work(): pl.pallas_call(functools.partial(local_kernel, n_py, scale), out_shape=(j...  18.3 us
    unnamed x26, local copies, waits for them, and re-layouts  10.5 us
    pallas_call x1, Pallas kernels, halo(): pl.pallas_call(functools.partial(halo_kernel, n_px, n_py), out_shape=(jax...  6.93 us
    pallas_call x1, Pallas kernels, new_block_of(): pl.pallas_call(masked_block_kernel, grid=(cap,), out_shape=jax.ShapeDtype...  4.69 us
  transfers between devices with their start and end apart: 1, of which 1 were waited for; matrix products, arithmetic and copies ran while one was open for 0% of the time, Pallas kernels for 2%

profile of v1, /device:TPU:0, one launch (start us, length us, event | category | flops | bytes accessed | tf_op | source)
XLA Modules:
  0.0 224.5 jit_solution(12233190982318967106)
XLA Ops:
  7.2 0.0 reduce-scatter.4.cloned.1.call-start
  7.2 0.0 copy-start
  7.2 1.4 copy-done
  8.6 0.0 copy-start.5
  8.6 0.9 copy-done.5
  9.5 0.0 copy-start.9
  9.5 0.7 copy-done.9
  10.2 0.0 copy-start.2
  10.2 0.0 copy-start.6
  10.2 6.9 %shard_map.103 = (f32[2,104,256]{2,1,0:T(8,128)S(1)}, f32[2,24,256]{2,1,0:T(8,128)S(1)}) custom-call(s32[8]{0:T(128)S(1)} %copy-done.9, f32[6,1,16,4096]{3,2,1,0:T(8,128)S(1)} %copy-done, f32[6,1,4096]{2,1,0:T(1,128)S(1)} %copy-done.5), custom_call_target="tpu_custom_call" | custom-call | tf_op jit(solution)/shard_map/pallas_call | solution.py:149
  17.1 0.0 copy-done.2
  17.1 0.0 copy-done.6
  17.1 0.0 copy-start.7
  17.1 0.7 copy-done.7
  17.8 18.3 %shard_map.104 = (f32[6,16,4096]{2,1,0:T(8,128)S(1)}, f32[32,16]{1,0:T(8,128)S(1)}, f32[48,2048]{1,0:T(8,128)S(1)}) custom-call(s32[8]{0:T(128)S(1)} %copy-done.9, f32[6,1,16,4096]{3,2,1,0:T(8,128)S(1)} %copy-done, f32[6,1,16,4096]{3,2,1,0:T(8,128)S(1)} %copy-done.2, f32[6,1,4096]{2,1,0:T(1,128)S(1)} %copy-done.5, s32[6,1,4096]{2,1,0:T(1,128)S(1)} %copy-done.6, ...), custom_call_target="tpu_custom_call" | custom-call | tf_op jit(solution)/shard_map/pallas_call | solution.py:303
  36.1 0.0 copy-start.3
  36.1 1.1 copy-done.3
  37.3 0.0 copy-start.1
  37.3 1.3 copy.15
  38.6 0.0 reduce-scatter.4.cloned.1.call-update
  38.6 0.8 copy.13.prev_ref
  39.4 41.3 %psum.14 = f32[32,16]{1,0:T(8,128)S(1)} all-reduce(f32[32,16]{1,0:T(8,128)S(1)} %get-tuple-element.12), channel_id=1, replica_groups=mesh['px'=8,'py'=4] {'px','py'}, use_global_device_ids=true, to_apply=%region_0.0 | all-reduce | flops 512 | bytes 4096 | tf_op jit(solution)/shard_map/psum | solution.py:434
  80.7 0.0 copy-done.1
  80.7 0.0 copy-start.4
  80.7 1.4 copy-done.4
  82.1 0.0 copy-start.10
  82.1 0.7 copy-done.10
  82.8 0.0 copy-start.8
  82.8 4.7 %shard_map.105 = f32[6,1,16,4096]{3,2,1,0:T(8,128)} custom-call(s32[8]{0:T(128)S(1)} %copy-done.10, f32[32,16]{1,0:T(8,128)S(1)} %broadcast_multiply_fusion.proj_ref, f32[6,1,16,4096]{3,2,1,0:T(8,128)S(1)} %copy-done.2, f32[6,1,16,4096]{3,2,1,0:T(8,128)S(1)} %copy-done.1, f32[6,16,4096]{2,1,0:T(8,128)S(1)} %copy-done.4), custom_call_target="tpu_custom_call" | custom-call | tf_op jit(solution)/shard_map/pallas_call | solution.py:346
  87.5 88.3 %reduce-scatter.4.cloned.1.call-done = f32[64,48]{1,0:T(8,128)} async-done(((f32[2048,48]{1,0:T(8,128)}), f32[64,48]{1,0:T(8,128)}) %reduce-scatter.4.cloned.1.call-update) | async-done | bytes 12304
  175.7 0.8 copy.16.sk_ref
  176.5 0.0 copy-done.8
  176.5 0.8 shard_map.106
  177.4 36.9 %psum.15.parts_ref = f32[32,48]{1,0:T(8,128)S(1)} all-reduce(f32[32,48]{1,0:T(8,128)S(1)} %get-tuple-element.16), channel_id=1, replica_groups=mesh['px'=8,'py'=4] {'px','py'}, use_global_device_ids=true, to_apply=%region_2.0 | all-reduce | flops 1536 | bytes 12288 | tf_op jit(solution)/shard_map/psum | solution.py:436
  214.3 2.7 %shard_map.107 = f32[32,16]{1,0:T(8,128)S(1)} custom-call(f32[32,48]{1,0:T(8,128)S(1)} %psum.15.parts_ref), custom_call_target="tpu_custom_call" | custom-call | tf_op jit(solution)/shard_map/pallas_call | solution.py:415
  217.0 0.7 copy.14
  (1 shorter events, 0.0 us)
Async XLA Ops:
  7.2 168.5 %reduce-scatter.4.cloned.1.call-start = ((), (), s32[]{:S(2)}) async-start(), calls=%async_computation.1 | async-start | bytes 1081344
  7.2 1.4 copy-start
  8.6 0.9 copy-start.5
  9.5 0.7 copy-start.9
  10.2 6.9 %copy-start.2 = (f32[6,1,16,4096]{3,2,1,0:T(8,128)S(1)}, f32[6,1,16,4096]{3,2,1,0:T(8,128)}, u32[]{:S(2)}) copy-start(f32[6,1,16,4096]{3,2,1,0:T(8,128)} %old_ref.3) | copy-start | bytes 4718596
  10.2 7.0 %copy-start.6 = (s32[6,1,4096]{2,1,0:T(1,128)S(1)}, s32[6,1,4096]{2,1,0:T(1,128)}, u32[]{:S(2)}) copy-start(s32[6,1,4096]{2,1,0:T(1,128)} %sgn_ref.1) | copy-start | bytes 294916
  17.1 0.7 copy-start.7
  36.1 1.1 copy-start.3
  37.3 43.4 %copy-start.1 = (f32[6,1,16,4096]{3,2,1,0:T(8,128)S(1)}, f32[6,1,16,4096]{3,2,1,0:T(8,128)}, u32[]{:S(2)}) copy-start(f32[6,1,16,4096]{3,2,1,0:T(8,128)} %last_ref.5) | copy-start | bytes 4718596
  80.7 1.4 copy-start.4
  82.1 0.7 copy-start.10
  82.8 93.8 %copy-start.8 = (f32[16,16]{1,0:T(8,128)S(1)}, f32[16,16]{1,0:T(8,128)}, u32[]{:S(2)}) copy-start(f32[16,16]{1,0:T(8,128)} %resid_ref.1) | copy-start | bytes 3076
Sparse Core Ops, SparseCore 0:
  38.7 136.9 reduce-scatter.3

commit v2 on v1

--- a/solution.py
+++ b/solution.py
@@ -258,14 +258,15 @@
             [whole[2 * rhs:3 * rhs], whole[5 * rhs:6 * rhs]], axis=0
         )
         both = lax.dot_general(
-            whole, imgs, (((1,), (1,)), ((), ())), preferred_element_type=f32
+            imgs, whole, (((1,), (1,)), ((), ())), preferred_element_type=f32
         )
-        both = both[:2 * rhs] + both[3 * rhs:5 * rhs]
-        return acc + both[:, :rhs] + both[:, rhs:]
-
-    gram_ref[...] = lax.fori_loop(0, cap, one_gram, jnp.zeros((2 * rhs, rhs), f32))
+        both = both[:, :2 * rhs] + both[:, 3 * rhs:5 * rhs]
+        return acc + both[:rhs] + both[rhs:]
+
+    gram_ref[...] = lax.fori_loop(0, cap, one_gram, jnp.zeros((rhs, 2 * rhs), f32))
 
     cell_bits = cells.bit_length() - 1
+    width = sketch_ref.shape[2]
     inner = lax.broadcasted_iota(jnp.int32, (TILE, TILE), 0)
     outer = cells // TILE
     hi_ids = lax.broadcasted_iota(jnp.int32, (outer, TILE), 0)
@@ -291,21 +292,23 @@
             total = total + w * (
                 spread[base:base + 3 * rhs] + spread[base + 3 * rhs:base + 6 * rhs]
             )
-        sketch_ref[:, at] = total * scale
+        total = total * scale
+        for r in range(TILE // width):
+            sketch_ref[t * (TILE // width) + r] = total[:, r * width:(r + 1) * width]
         return carry
 
     lax.fori_loop(0, rows_ref.shape[1] // TILE, one_tile, 0)
 
 
-def local_work(n_py, scale, counts, last, old, kap, sgn, yg, xg, rows):
+def local_work(n_px, n_py, scale, counts, last, old, kap, sgn, yg, xg, rows):
     cap, _, rhs, cells = last.shape
     k = rows.shape[1]
     return pl.pallas_call(
         functools.partial(local_kernel, n_py, scale),
         out_shape=(
             jax.ShapeDtypeStruct((cap, rhs, cells), f32),
-            jax.ShapeDtypeStruct((2 * rhs, rhs), f32),
-            jax.ShapeDtypeStruct((3 * rhs, k), f32),
+            jax.ShapeDtypeStruct((rhs, 2 * rhs), f32),
+            jax.ShapeDtypeStruct((n_px, 3 * rhs, k // n_px), f32),
         ),
         in_specs=[SMEM] + [VMEM] * 7,
         out_specs=(VMEM, VMEM, VMEM),
@@ -322,7 +325,7 @@
     proj = proj_ref[...]
     pair = jnp.concatenate([old_ref[0, 0], last_ref[0, 0]], axis=0)
     moved = lax.dot_general(
-        proj, pair, (((0,), (0,)), ((), ())), precision=highest, preferred_element_type=f32
+        proj, pair, (((1,), (0,)), ((), ())), precision=highest, preferred_element_type=f32
     )
     out_ref[0, 0] = image_ref[0] - moved
 
@@ -371,28 +374,6 @@
     )
 
 
-def normal_kernel(rhs, sk_ref, proj_ref, prev_ref, resid_ref, mine_ref, parts_ref):
-    pair = sk_ref[pl.ds(0, 2 * rhs), :]
-    second = sk_ref[pl.ds(2 * rhs, rhs), :]
-    mine_ref[pl.ds(0, 2 * rhs), :] = pair
-    mine_ref[pl.ds(2 * rhs, rhs), :] = second - tn(proj_ref[...], pair)
-    images = jnp.concatenate([tn(prev_ref[...], pair), second], axis=0)
-    target = tn(resid_ref[...], pair[:rhs])
-    parts_ref[...] = nt(images, jnp.concatenate([images, target], axis=0))
-
-
-def normal_parts(sk, proj, prev, resid):
-    rhs = resid.shape[0]
-    return pl.pallas_call(
-        functools.partial(normal_kernel, rhs),
-        out_shape=(
-            jax.ShapeDtypeStruct(sk.shape, f32),
-            jax.ShapeDtypeStruct((2 * rhs, 3 * rhs), f32),
-        ),
-        compiler_params=params(),
-    )(sk, proj, prev, resid)
-
-
 def eliminate(work):
     size, width = work.shape
     row_id = lax.broadcasted_iota(jnp.int32, (size, 1), 0)
@@ -405,18 +386,115 @@
     return work
 
 
-def solve_kernel(parts_ref, out_ref):
-    size = parts_ref.shape[0]
-    out_ref[...] = eliminate(parts_ref[...])[:, size:]
-
-
-def solve(parts):
-    size, width = parts.shape
+def nn(left, right):
+    return jnp.dot(left, right, precision=highest, preferred_element_type=f32)
+
+
+def reduce_kernel(
+    n_px, n_py, total_cells, gram_ref, sketch_ref, prev_ref, resid_ref, proj_ref, mine_ref,
+    answer_ref, gram_x, sketch_x, gram_y, sketch_y, parts_x, gram_xs, gram_xr, sketch_xs,
+    sketch_xr, gram_ys, gram_yr, sketch_ys, sketch_yr, parts_s, parts_r,
+):
+    i = lax.axis_index("px")
+    j = lax.axis_index("py")
+    rhs = resid_ref.shape[0]
+    x_peers = [lax.rem(i + d, n_px) for d in range(1, n_px)]
+    y_peers = [lax.rem(j + d, n_py) for d in range(1, n_py)]
+    barrier = pltpu.get_barrier_semaphore()
+    for axis, peers in (("px", x_peers), ("py", y_peers)):
+        for peer in peers:
+            pl.semaphore_signal(
+                barrier, inc=1, device_id={axis: peer}, device_id_type=pl.DeviceIdType.MESH
+            )
+    pl.semaphore_wait(barrier, n_px + n_py - 2)
+
+    def exchange(axis, me, peers, source, slots, send, recv):
+        def copy(peer, slot):
+            return pltpu.make_async_remote_copy(
+                src_ref=source(peer),
+                dst_ref=slots.at[slot],
+                send_sem=send.at[peer],
+                recv_sem=recv.at[slot],
+                device_id={axis: peer},
+                device_id_type=pl.DeviceIdType.MESH,
+            )
+
+        for peer in peers:
+            copy(peer, me).start()
+
+        def finish():
+            for peer in peers:
+                copy(peer, peer).wait_recv()
+            for peer in peers:
+                copy(peer, me).wait_send()
+
+        return finish
+
+    def total(slots):
+        acc = slots[0]
+        for p in range(1, slots.shape[0]):
+            acc = acc + slots[p]
+        return acc
+
+    gram_done = exchange("px", i, x_peers, lambda p: gram_ref, gram_x, gram_xs, gram_xr)
+    sketch_done = exchange(
+        "px", i, x_peers, lambda p: sketch_ref.at[p], sketch_x, sketch_xs, sketch_xr
+    )
+    gram_x[i] = gram_ref[...]
+    sketch_x[i] = sketch_ref[i]
+    gram_done()
+    gram_y[j] = total(gram_x)
+    gram_done = exchange("py", j, y_peers, lambda p: gram_y.at[j], gram_y, gram_ys, gram_yr)
+    sketch_done()
+    sketch_y[j] = total(sketch_x)
+    sketch_done = exchange("py", j, y_peers, lambda p: sketch_y.at[j], sketch_y, sketch_ys, sketch_yr)
+    gram_done()
+    proj = total(gram_y) * (1.0 / total_cells)
+    proj_ref[...] = proj
+    sketch_done()
+    whole = total(sketch_y)
+    pair = whole[:2 * rhs]
+    second = whole[2 * rhs:]
+    images = jnp.concatenate([tn(prev_ref[...], pair), second], axis=0)
+    target = tn(resid_ref[...], pair[:rhs])
+    parts_x[i] = nt(images, jnp.concatenate([images, target], axis=0))
+    parts_done = exchange("px", i, x_peers, lambda p: parts_x.at[i], parts_x, parts_s, parts_r)
+    newer = second - nn(proj, pair)
+    width, share = whole.shape[1], mine_ref.shape[1]
+    chosen = (
+        lax.broadcasted_iota(jnp.int32, (width, share), 0)
+        == lax.broadcasted_iota(jnp.int32, (width, share), 1) + j * share
+    ).astype(f32)
+    mine_ref[...] = nn(jnp.concatenate([pair, newer], axis=0), chosen)
+    parts_done()
+    answer_ref[...] = eliminate(total(parts_x))[:, 2 * rhs:]
+
+
+def reduce_work(n_px, n_py, total_cells, gram, sketch, prev, resid):
+    rhs = resid.shape[0]
+    width = sketch.shape[2]
+    sems = lambda n: pltpu.SemaphoreType.DMA((n,))
     return pl.pallas_call(
-        solve_kernel,
-        out_shape=jax.ShapeDtypeStruct((size, width - size), f32),
-        compiler_params=params(),
-    )(parts)
+        functools.partial(reduce_kernel, n_px, n_py, total_cells),
+        out_shape=(
+            jax.ShapeDtypeStruct(gram.shape, f32),
+            jax.ShapeDtypeStruct((3 * rhs, width // n_py), f32),
+            jax.ShapeDtypeStruct((2 * rhs, rhs), f32),
+        ),
+        in_specs=[VMEM] * 4,
+        out_specs=(VMEM, VMEM, VMEM),
+        scratch_shapes=[
+            pltpu.VMEM((n_px,) + gram.shape, f32),
+            pltpu.VMEM(sketch.shape, f32),
+            pltpu.VMEM((n_py,) + gram.shape, f32),
+            pltpu.VMEM((n_py,) + sketch.shape[1:], f32),
+            pltpu.VMEM((n_px, 2 * rhs, 3 * rhs), f32),
+            sems(n_px), sems(n_px), sems(n_px), sems(n_px),
+            sems(n_py), sems(n_py), sems(n_py), sems(n_py),
+            sems(n_px), sems(n_px),
+        ],
+        compiler_params=params(collective_id=1, has_side_effects=True),
+    )(gram, sketch, prev, resid)
 
 
 def body(
@@ -427,13 +505,12 @@
     rows = sample_rows.reshape(1, -1)
     yg, xg = halo(n_px, n_py, counts, basis_last, coefficient)
     image, gram, sketch = local_work(
-        n_py, 1.0 / math.sqrt(total_cells), counts, basis_last, basis_old, coefficient, signs, yg,
-        xg, rows,
-    )
-    sketch_share = lax.psum_scatter(sketch, ("px", "py"), scatter_dimension=1, tiled=True)
-    proj = lax.psum(gram, ("px", "py")) / total_cells
-    mine, parts = normal_parts(sketch_share, proj, previous_coef, residual_factor)
-    answer = solve(lax.psum(parts, ("px", "py")))
+        n_px, n_py, 1.0 / math.sqrt(total_cells), counts, basis_last, basis_old, coefficient, signs,
+        yg, xg, rows,
+    )
+    proj, mine, answer = reduce_work(
+        n_px, n_py, total_cells, gram, sketch, previous_coef, residual_factor
+    )
     new_block = new_block_of(counts, proj, basis_old, basis_last, image)
     return (new_block, mine, answer)
 

time: 226 us -> 62.4 us (0.28)
  waiting for transfers between devices: 88.3 us -> 0 us
  blocking collectives: 78.2 us -> 0 us
  Pallas kernels: 33.4 us -> 56.2 us
  between operations: 14.1 us -> 0.72 us
  local copies, waits for them, and re-layouts: 10.5 us -> 5.03 us
    unnamed x2 -> x0, waiting for transfers between devices: 88.3 us -> none
    psum x2 -> x0, blocking collectives: 78.2 us -> none  [the longest x1 41.3 us: body(): proj = lax.psum(gram, ('px', 'py')) / total_cells]
    pallas_call x2 -> x1, Pallas kernels: 3.53 us -> 27.4 us  [reduce_work(): pl.pallas_call(functools.partial(reduce_kernel, n_px, n_py, total_cells),...]
    unnamed x26 -> x19, local copies, waits for them, and re-layouts: 10.5 us -> 5.03 us
  transfers between devices with their start and end apart: 1 -> 0, of which waited for: 1 -> 0; matrix products, arithmetic and copies ran while one was open for 0% -> 0% of each run, Pallas kernels for 2% -> 0%
where the time goes in v2:
time: 62.4 us; the launch traced here: 62 us
  Pallas kernels  56.2 us (90%)
  local copies, waits for them, and re-layouts  5.03 us (8%)
  between operations  0.72 us (1%)
    pallas_call x1, Pallas kernels, reduce_work(): pl.pallas_call(functools.partial(reduce_kernel, n_px, n_py, total_cells),...  27.4 us
    pallas_call x1, Pallas kernels, local_work(): pl.pallas_call(functools.partial(local_kernel, n_py, scale), out_shape=(j...  18.6 us
    pallas_call x1, Pallas kernels, halo(): pl.pallas_call(functools.partial(halo_kernel, n_px, n_py), out_shape=(jax...  6.93 us
    unnamed x19, local copies, waits for them, and re-layouts  5.03 us
    pallas_call x1, Pallas kernels, new_block_of(): pl.pallas_call(masked_block_kernel, grid=(cap,), out_shape=jax.ShapeDtype...  3.29 us

profile of v2, /device:TPU:0, one launch (start us, length us, event | category | flops | bytes accessed | tf_op | source)
XLA Modules:
  0.0 62.0 jit_solution(8152382732596201383)
XLA Ops:
  0.6 0.0 copy-start.5
  0.6 0.8 %copy.11.prev_ref = f32[32,16]{1,0:T(8,128)S(1)} copy(f32[32,16]{0,1:T(8,128)} %param.14) | data formatting | bytes 4096 | tf_op args[6]
  1.4 0.0 copy-start
  1.4 1.4 %copy-done = f32[6,1,16,4096]{3,2,1,0:T(8,128)S(1)} copy-done((f32[6,1,16,4096]{3,2,1,0:T(8,128)S(1)}, f32[6,1,16,4096]{3,2,1,0:T(8,128)}, u32[]{:S(2)}) %copy-start) | copy-done | bytes 1572888
  2.8 0.0 copy-start.3
  2.8 0.9 %copy-done.3 = f32[6,1,4096]{2,1,0:T(1,128)S(1)} copy-done((f32[6,1,4096]{2,1,0:T(1,128)S(1)}, f32[6,1,4096]{2,1,0:T(1,128)}, u32[]{:S(2)}) %copy-start.3) | copy-done | bytes 98328
  3.7 0.0 copy-start.7
  3.7 0.7 %copy-done.7 = s32[8]{0:T(128)S(1)} copy-done((s32[8]{0:T(128)S(1)}, s32[8]{0:T(128)}, u32[]{:S(2)}) %copy-start.7) | copy-done | bytes 56
  4.4 0.0 copy-start.2
  4.4 0.0 copy-start.4
  4.4 6.9 %shard_map.103 = (f32[2,104,256]{2,1,0:T(8,128)S(1)}, f32[2,24,256]{2,1,0:T(8,128)S(1)}) custom-call(s32[8]{0:T(128)S(1)} %copy-done.7, f32[6,1,16,4096]{3,2,1,0:T(8,128)S(1)} %copy-done, f32[6,1,4096]{2,1,0:T(1,128)S(1)} %copy-done.3), custom_call_target="tpu_custom_call" | custom-call | tf_op jit(solution)/shard_map/pallas_call | solution.py:149
  11.3 0.0 copy-done.5
  11.3 0.0 copy-done.2
  11.3 0.0 copy-done.4
  11.3 0.0 copy-start.6
  11.4 0.0 copy-start.1
  11.4 18.6 %shard_map.104 = (f32[6,16,4096]{2,1,0:T(8,128)S(1)}, f32[16,32]{1,0:T(8,128)S(1)}, f32[8,48,256]{2,1,0:T(8,128)S(1)}) custom-call(s32[8]{0:T(128)S(1)} %copy-done.7, f32[6,1,16,4096]{3,2,1,0:T(8,128)S(1)} %copy-done, f32[6,1,16,4096]{3,2,1,0:T(8,128)S(1)} %copy-done.2, f32[6,1,4096]{2,1,0:T(1,128)S(1)} %copy-done.3, s32[6,1,4096]{2,1,0:T(1,128)S(1)} %copy-done.4, ...), custom_call_target="tpu_custom_call" | custom-call | tf_op jit(solution)/shard_map/pallas_call | solution.py:306
  30.0 0.0 copy-done.6
  30.0 27.4 %shard_map.105 = (f32[16,32]{1,0:T(8,128)S(1)}, f32[48,64]{1,0:T(8,128)S(1)}, f32[32,16]{1,0:T(8,128)S(1)}) custom-call(f32[16,32]{1,0:T(8,128)S(1)} %get-tuple-element.13.gram_ref, f32[8,48,256]{2,1,0:T(8,128)S(1)} %get-tuple-element.14.sketch_ref, f32[32,16]{1,0:T(8,128)S(1)} %copy.11.prev_ref, f32[16,16]{1,0:T(8,128)S(1)} %copy-done.6), custom_call_target="tpu_custom_call" | custom-call | tf_op jit(solution)/shard_map/pallas_call | solution.py:477
  57.4 0.0 copy-done.1
  57.4 3.3 %shard_map.106 = f32[6,1,16,4096]{3,2,1,0:T(8,128)} custom-call(s32[8]{0:T(128)S(1)} %copy-done.7, f32[16,32]{1,0:T(8,128)S(1)} %get-tuple-element.15.proj_ref, f32[6,1,16,4096]{3,2,1,0:T(8,128)S(1)} %copy-done.2, f32[6,1,16,4096]{3,2,1,0:T(8,128)S(1)} %copy-done.1, f32[6,16,4096]{2,1,0:T(8,128)S(1)} %get-tuple-element.16.image_ref), custom_call_target="tpu_custom_call" | custom-call | tf_op jit(solution)/shard_map/pallas_call | solution.py:349
  60.7 0.7 %copy.12 = f32[32,16]{0,1:T(8,128)} copy(f32[32,16]{1,0:T(8,128)S(1)} %get-tuple-element.21) | data formatting | bytes 4096
  61.4 0.6 copy.14
Async XLA Ops:
  0.6 10.7 %copy-start.5 = (s32[2048]{0:T(1024)S(1)}, s32[2048]{0:T(1024)}, u32[]{:S(2)}) copy-start(s32[2048]{0:T(1024)} %param.15) | copy-start | bytes 24580
  1.4 1.4 %copy-start = (f32[6,1,16,4096]{3,2,1,0:T(8,128)S(1)}, f32[6,1,16,4096]{3,2,1,0:T(8,128)}, u32[]{:S(2)}) copy-start(f32[6,1,16,4096]{3,2,1,0:T(8,128)} %last_ref.5) | copy-start | bytes 4718596
  2.8 0.9 %copy-start.3 = (f32[6,1,4096]{2,1,0:T(1,128)S(1)}, f32[6,1,4096]{2,1,0:T(1,128)}, u32[]{:S(2)}) copy-start(f32[6,1,4096]{2,1,0:T(1,128)} %kap_ref.3) | copy-start | bytes 294916
  3.7 0.7 %copy-start.7 = (s32[8]{0:T(128)S(1)}, s32[8]{0:T(128)}, u32[]{:S(2)}) copy-start(s32[8]{0:T(128)} %counts_ref.5) | copy-start | bytes 100
  4.4 7.0 %copy-start.2 = (f32[6,1,16,4096]{3,2,1,0:T(8,128)S(1)}, f32[6,1,16,4096]{3,2,1,0:T(8,128)}, u32[]{:S(2)}) copy-start(f32[6,1,16,4096]{3,2,1,0:T(8,128)} %old_ref.3) | copy-start | bytes 4718596
  4.4 7.0 %copy-start.4 = (s32[6,1,4096]{2,1,0:T(1,128)S(1)}, s32[6,1,4096]{2,1,0:T(1,128)}, u32[]{:S(2)}) copy-start(s32[6,1,4096]{2,1,0:T(1,128)} %sgn_ref.1) | copy-start | bytes 294916
  11.3 18.6 %copy-start.6 = (f32[16,16]{1,0:T(8,128)S(1)}, f32[16,16]{1,0:T(8,128)}, u32[]{:S(2)}) copy-start(f32[16,16]{1,0:T(8,128)} %resid_ref.1) | copy-start | bytes 3076
  11.4 46.1 %copy-start.1 = (f32[6,1,16,4096]{3,2,1,0:T(8,128)S(1)}, f32[6,1,16,4096]{3,2,1,0:T(8,128)}, u32[]{:S(2)}) copy-start(f32[6,1,16,4096]{3,2,1,0:T(8,128)} %last_ref.5) | copy-start | bytes 4718596

commit v3 on v1

v3 whole, which is shorter than its diff:
```python
import functools
import math

import jax
import jax.numpy as jnp
from jax import lax
from jax.experimental import pallas as pl
from jax.experimental.pallas import tpu as pltpu
from jax.sharding import PartitionSpec as P

PS = 16
MEANX = 2
TILE = 256

highest = lax.Precision.HIGHEST
f32 = jnp.float32
bf16 = jnp.bfloat16
VMEM = pl.BlockSpec(memory_space=pltpu.VMEM)
SMEM = pl.BlockSpec(memory_space=pltpu.SMEM)


def params(**more):
    return pltpu.CompilerParams(vmem_limit_bytes=48 * 1024 * 1024, **more)


def parity_sign(values, bits):
    amount = 1
    while amount < bits:
        amount *= 2
    while amount > 1:
        amount //= 2
        values = jnp.bitwise_xor(values, jnp.right_shift(values, amount))
    return 1 - 2 * jnp.bitwise_and(values, 1)


def split(values):
    head = values.astype(bf16)
    return head, (values - head.astype(f32)).astype(bf16)


def tn(left, right):
    return lax.dot_general(
        left, right, (((0,), (0,)), ((), ())), precision=highest, preferred_element_type=f32
    )


def nt(left, right):
    return lax.dot_general(
        left, right, (((1,), (1,)), ((), ())), precision=highest, preferred_element_type=f32
    )


def eliminate(work):
    size, width = work.shape
    row_id = lax.broadcasted_iota(jnp.int32, (size, 1), 0)
    for step in range(size):
        row = work[step:step + 1, :]
        pivot = row[:, step:step + 1]
        scaled = row / pivot
        column = jnp.where(row_id == step, 0.0, work[:, step:step + 1])
        work = jnp.where(row_id == step, scaled, work - column * scaled)
    return work


def nn(left, right):
    return jnp.dot(left, right, precision=highest, preferred_element_type=f32)


def step_kernel(
    n_px, n_py, total_cells, counts_ref, last_hbm, old_hbm, kap_hbm, sgn_hbm, rows_ref, prev_ref,
    resid_ref, new_hbm, mine_ref, answer_ref, last_ref, old_ref, kap_ref, sgn_ref, in_sem, out_sem,
    xbuf, ybuf, xg_ref, yg_ref, xsend, xrecv, ysend, yrecv, image_ref, cols, table, gram_ref,
    sketch_ref, gram_x, sketch_x, gram_y, sketch_y, parts_x, gram_xs, gram_xr, sketch_xs,
    sketch_xr, gram_ys, gram_yr, sketch_ys, sketch_yr, parts_s, parts_r,
):
    i = lax.axis_index("px")
    j = lax.axis_index("py")
    cap, _, rhs, cells = last_ref.shape
    plane = PS * PS
    top = (PS - 1) * plane
    mesh_id = pl.DeviceIdType.MESH
    loads = [
        pltpu.make_async_copy(source, target, in_sem.at[index])
        for index, (source, target) in enumerate(
            ((last_hbm, last_ref), (kap_hbm, kap_ref), (old_hbm, old_ref), (sgn_hbm, sgn_ref))
        )
    ]
    for load in loads:
        load.start()
    x_peers = [lax.rem(i + d, n_px) for d in range(1, n_px)]
    y_peers = [lax.rem(j + d, n_py) for d in range(1, n_py)]
    barrier = pltpu.get_barrier_semaphore()
    for axis, peers in (("px", x_peers), ("py", y_peers)):
        for peer in peers:
            pl.semaphore_signal(barrier, inc=1, device_id={axis: peer}, device_id_type=mesh_id)
    around = [
        ("py", j - 1, j > 0),
        ("py", j + 1, j < n_py - 1),
        ("px", i - 1, i > 0),
        ("px", i + 1, i < n_px - 1),
    ]
    lane = lax.broadcasted_iota(jnp.int32, (1, plane), 1)
    b_id = lane // PS
    c_id = lane % PS
    held = counts_ref[i]
    offset = jnp.int32(0)
    for t in range(n_px):
        offset = offset + jnp.where(t < i, counts_ref[t], 0)
    tail = jnp.clip(held - 1, 0, cap - 1)

    loads[0].wait()
    loads[1].wait()
    xbuf[0, pl.ds(0, rhs), :] = last_ref[0, 0, :, pl.ds(0, plane)]
    xbuf[0, pl.ds(rhs, 1), :] = kap_ref[0, :, pl.ds(0, plane)]
    xbuf[1, pl.ds(0, rhs), :] = last_ref[tail, 0, :, pl.ds(top, plane)]
    xbuf[1, pl.ds(rhs, 1), :] = kap_ref[tail, :, pl.ds(top, plane)]

    def pack(s, carry):
        u0 = jnp.zeros((rhs, plane), f32)
        u1 = jnp.zeros((rhs, plane), f32)
        k0 = jnp.zeros((1, plane), f32)
        k1 = jnp.zeros((1, plane), f32)
        for a in range(PS):
            mine = b_id == a
            u = last_ref[s, 0, :, pl.ds(a * plane, plane)]
            k = kap_ref[s, :, pl.ds(a * plane, plane)]
            lo = (a * PS) % plane
            hi = (a * PS + PS) % plane
            u0 = jnp.where(mine, pltpu.roll(u, lo, 1) if lo else u, u0)
            u1 = jnp.where(mine, pltpu.roll(u, hi, 1) if hi else u, u1)
            k0 = jnp.where(mine, pltpu.roll(k, lo, 1) if lo else k, k0)
            k1 = jnp.where(mine, pltpu.roll(k, hi, 1) if hi else k, k1)
        ybuf[0, pl.ds(pl.multiple_of(s * rhs, 8), rhs), :] = u0
        ybuf[1, pl.ds(pl.multiple_of(s * rhs, 8), rhs), :] = u1
        ybuf[0, pl.ds(cap * rhs + s, 1), :] = k0
        ybuf[1, pl.ds(cap * rhs + s, 1), :] = k1
        return carry

    faces = {0: (ybuf, yg_ref, ysend, yrecv), 2: (xbuf, xg_ref, xsend, xrecv)}

    def face_copy(base, side, ghost_side):
        axis, index, _ = around[base + side]
        buf, ghost, send, recv = faces[base]
        return pltpu.make_async_remote_copy(
            src_ref=buf.at[side],
            dst_ref=ghost.at[ghost_side],
            send_sem=send.at[side],
            recv_sem=recv.at[ghost_side],
            device_id={axis: index},
            device_id_type=mesh_id,
        )

    def when_near(base, side, action):
        @pl.when(around[base + side][2])
        def _():
            action()

    pl.semaphore_wait(barrier, n_px + n_py - 2)
    for side in range(2):
        when_near(2, side, lambda: face_copy(2, side, 1 - side).start())
    lax.fori_loop(0, cap, pack, 0)
    for side in range(2):
        when_near(0, side, lambda: face_copy(0, side, 1 - side).start())
    for base in (0, 2):
        for side in range(2):
            @pl.when(jnp.logical_not(around[base + side][2]))
            def _():
                ghost = faces[base][1]
                ghost[side] = jnp.zeros(ghost.shape[1:], f32)

    loads[2].wait()
    loads[3].wait()

    def flips(s, at):
        return jnp.where(s < held, 1 - 2 * sgn_ref[s, :, at], 0).astype(f32)

    def keep(s, part, at, value):
        first_part, rest = split(value)
        cols[s, pl.ds(part * rhs, rhs), at] = first_part
        cols[s, pl.ds((part + 3) * rhs, rhs), at] = rest

    def pair_columns(s, carry):
        for a in range(PS):
            at = pl.ds(a * plane, plane)
            sg = flips(s, at)
            keep(s, 0, at, old_ref[s, 0, :, at] * sg)
            keep(s, 1, at, last_ref[s, 0, :, at] * sg)
        return carry

    lax.fori_loop(0, cap, pair_columns, 0)

    for base in (2, 0):
        for side in range(2):
            when_near(base, side, lambda: face_copy(base, side, 1 - side).wait_send())
            when_near(base, side, lambda: face_copy(base, side, side).wait_recv())

    def operate(s, carry):
        live = s < held
        first = s == 0
        final = s == held - 1
        before = jnp.maximum(s - 1, 0)
        after = jnp.minimum(s + 1, cap - 1)
        ks = pl.ds(cap * rhs + s, 1)
        us = pl.ds(pl.multiple_of(s * rhs, 8), rhs)
        kg_lo, kg_hi = yg_ref[0, ks, :], yg_ref[1, ks, :]
        ug_lo, ug_hi = yg_ref[0, us, :], yg_ref[1, us, :]
        for a in range(PS):
            at = pl.ds(a * plane, plane)

            def planes(ref_at, ghost_rows):
                if a == 0:
                    low = jnp.where(first, xg_ref[0, ghost_rows, :], ref_at(before, top))
                else:
                    low = ref_at(s, (a - 1) * plane)
                if a == PS - 1:
                    high = jnp.where(final, xg_ref[1, ghost_rows, :], ref_at(after, 0))
                else:
                    high = ref_at(s, (a + 1) * plane)
                return low, high

            def rolled(value, glo, ghi):
                lo = (plane - a * PS) % plane
                hi = (plane - PS - a * PS) % plane
                blo = jnp.where(
                    b_id == 0, pltpu.roll(glo, lo, 1) if lo else glo, pltpu.roll(value, PS, 1)
                )
                bhi = jnp.where(
                    b_id == PS - 1,
                    pltpu.roll(ghi, hi, 1) if hi else ghi,
                    pltpu.roll(value, plane - PS, 1),
                )
                return blo, bhi, pltpu.roll(value, 1, 1), pltpu.roll(value, plane - 1, 1)

            k = kap_ref[s, :, at]
            u = last_ref[s, 0, :, at]
            ka = planes(lambda t, p: kap_ref[t, :, pl.ds(p, plane)], pl.ds(rhs, 1))
            ua = planes(lambda t, p: last_ref[t, 0, :, pl.ds(p, plane)], pl.ds(0, rhs))
            kr = rolled(k, kg_lo, kg_hi)
            ur = rolled(u, ug_lo, ug_hi)
            kc = (jnp.where(c_id == 0, 0.0, kr[2]), jnp.where(c_id == PS - 1, 0.0, kr[3]))
            near_k = (ka[0], ka[1], kr[0], kr[1], kc[0], kc[1])
            near_u = (ua[0], ua[1]) + ur
            weights = [0.5 * (k + kn) for kn in near_k]
            diag = weights[0]
            for w in weights[1:]:
                diag = diag + w
            weights[4] = jnp.where(c_id == 0, 0.0, weights[4])
            weights[5] = jnp.where(c_id == PS - 1, 0.0, weights[5])
            image = diag * u
            for w, un in zip(weights, near_u):
                image = image - w * un
            image = jnp.where(live, image, 0.0)
            image_ref[s, 0, :, at] = image
            keep(s, 2, at, image * flips(s, at))
        return carry

    lax.fori_loop(0, cap, operate, 0)

    def one_gram(s, acc):
        whole = cols[s]
        imgs = jnp.concatenate([whole[2 * rhs:3 * rhs], whole[5 * rhs:6 * rhs]], axis=0)
        both = lax.dot_general(
            imgs, whole, (((1,), (1,)), ((), ())), preferred_element_type=f32
        )
        both = both[:, :2 * rhs] + both[:, 3 * rhs:5 * rhs]
        return acc + both[:rhs] + both[rhs:]

    gram_ref[...] = lax.fori_loop(0, cap, one_gram, jnp.zeros((rhs, 2 * rhs), f32))

    def mover(axis, source, slots, send, recv):
        def copy(peer, slot):
            return pltpu.make_async_remote_copy(
                src_ref=source(peer),
                dst_ref=slots.at[slot],
                send_sem=send.at[peer],
                recv_sem=recv.at[slot],
                device_id={axis: peer},
                device_id_type=mesh_id,
            )

        return copy

    def start(copy, me, peers):
        for peer in peers:
            copy(peer, me).start()

    def finish(copy, me, peers):
        for peer in peers:
            copy(peer, peer).wait_recv()
        for peer in peers:
            copy(peer, me).wait_send()

    def total(slots):
        acc = slots[0]
        for p in range(1, slots.shape[0]):
            acc = acc + slots[p]
        return acc

    gram_x_copy = mover("px", lambda p: gram_ref, gram_x, gram_xs, gram_xr)
    gram_y_copy = mover("py", lambda p: gram_y.at[j], gram_y, gram_ys, gram_yr)
    sketch_x_copy = mover("px", lambda p: sketch_ref.at[p], sketch_x, sketch_xs, sketch_xr)
    sketch_y_copy = mover("py", lambda p: sketch_y.at[j], sketch_y, sketch_ys, sketch_yr)
    parts_copy = mover("px", lambda p: parts_x.at[i], parts_x, parts_s, parts_r)

    start(gram_x_copy, i, x_peers)
    gram_x[i] = gram_ref[...]

    cell_bits = cells.bit_length() - 1
    width = sketch_ref.shape[2]
    per = TILE // width
    inner = lax.broadcasted_iota(jnp.int32, (TILE, TILE), 0)
    outer = cells // TILE
    hi_ids = lax.broadcasted_iota(jnp.int32, (outer, TILE), 0)
    tiles = rows_ref.shape[1] // TILE
    scale = 1.0 / math.sqrt(total_cells)

    def one_tile(turn, carry):
        t = lax.rem(i // per + 1 + turn, tiles)
        at = pl.ds(pl.multiple_of(t * TILE, TILE), TILE)
        rows = rows_ref[:, at]
        inside = parity_sign(jnp.bitwise_and(inner, rows), 8).astype(f32).astype(bf16)
        across = parity_sign(
            jnp.bitwise_and(hi_ids, jnp.right_shift(rows, 8) & (outer - 1)), 4
        ).astype(f32)
        for h in range(outer):
            table[pl.ds(h * TILE, TILE), :] = inside * across[h:h + 1].astype(bf16)
        flat = cols[...].reshape(cap * 6 * rhs, cells)
        spread = jnp.dot(flat, table[...], preferred_element_type=f32)
        summed = jnp.zeros((3 * rhs, TILE), f32)
        for s in range(cap):
            patch = (offset + s) * n_py + j
            w = parity_sign(
                jnp.bitwise_and(jnp.right_shift(rows, cell_bits), patch), 16
            ).astype(f32)
            base = s * 6 * rhs
            summed = summed + w * (
                spread[base:base + 3 * rhs] + spread[base + 3 * rhs:base + 6 * rhs]
            )
        summed = summed * scale
        for r in range(per):
            owner = t * per + r
            sketch_ref[owner] = summed[:, r * width:(r + 1) * width]

            @pl.when(owner != i)
            def _():
                sketch_x_copy(owner, i).start()
        return carry

    half = tiles // 2
    lax.fori_loop(0, half, one_tile, 0)
    finish(gram_x_copy, i, x_peers)
    gram_y[j] = total(gram_x)
    start(gram_y_copy, j, y_peers)
    lax.fori_loop(half, tiles, one_tile, 0)
    sketch_x[i] = sketch_ref[i]
    finish(gram_y_copy, j, y_peers)
    proj = total(gram_y) * (1.0 / total_cells)
    finish(sketch_x_copy, i, x_peers)
    sketch_y[j] = total(sketch_x)
    start(sketch_y_copy, j, y_peers)

    proj_head, proj_rest = split(proj)
    none = jnp.zeros((rhs, rhs), bf16)
    both_proj = jnp.concatenate(
        [
            jnp.concatenate([proj_head, none, proj_head, none], axis=1),
            jnp.concatenate([proj_rest, none, jnp.zeros((rhs, 3 * rhs), bf16)], axis=1),
        ],
        axis=0,
    )

    def store_of(s):
        return pltpu.make_async_copy(image_ref.at[s], new_hbm.at[s], out_sem.at[s])

    def one_block(s, carry):
        moved = jnp.dot(both_proj, cols[s], preferred_element_type=f32)
        moved = moved[:rhs] + moved[rhs:]
        image_ref[s, 0] = image_ref[s, 0] - moved * flips(s, pl.ds(0, cells))
        store_of(s).start()
        return carry

    lax.fori_loop(0, cap // 2, one_block, 0)
    finish(sketch_y_copy, j, y_peers)
    whole = total(sketch_y)
    pair = whole[:2 * rhs]
    second = whole[2 * rhs:]
    images = jnp.concatenate([tn(prev_ref[...], pair), second], axis=0)
    target = tn(resid_ref[...], pair[:rhs])
    parts_x[i] = nt(images, jnp.concatenate([images, target], axis=0))
    start(parts_copy, i, x_peers)
    lax.fori_loop(cap // 2, cap, one_block, 0)
    newer = second - nn(proj, pair)
    share = mine_ref.shape[1]
    chosen = (
        lax.broadcasted_iota(jnp.int32, (width, share), 0)
        == lax.broadcasted_iota(jnp.int32, (width, share), 1) + j * share
    ).astype(f32)
    mine_ref[...] = nn(jnp.concatenate([pair, newer], axis=0), chosen)
    finish(parts_copy, i, x_peers)
    answer_ref[...] = eliminate(total(parts_x))[:, 2 * rhs:]
    for s in range(cap):
        store_of(s).wait()


def step(n_px, n_py, total_cells, counts, last, old, kap, sgn, rows, prev, resid):
    cap, _, rhs, cells = last.shape
    width = rows.shape[1] // n_px
    plane = PS * PS
    yrows = cap * rhs + -(-cap // 8) * 8
    xrows = rhs + 8
    hbm = pl.BlockSpec(memory_space=pl.ANY)
    sems = lambda n: pltpu.SemaphoreType.DMA((n,))
    return pl.pallas_call(
        functools.partial(step_kernel, n_px, n_py, total_cells),
        out_shape=(
            jax.ShapeDtypeStruct(last.shape, f32),
            jax.ShapeDtypeStruct((3 * rhs, width // n_py), f32),
            jax.ShapeDtypeStruct((2 * rhs, rhs), f32),
        ),
        in_specs=[SMEM] + [hbm] * 4 + [VMEM] * 3,
        out_specs=(hbm, VMEM, VMEM),
        scratch_shapes=[
            pltpu.VMEM(last.shape, f32),
            pltpu.VMEM(old.shape, f32),
            pltpu.VMEM(kap.shape, f32),
            pltpu.VMEM(sgn.shape, jnp.int32),
            sems(4), sems(cap),
            pltpu.VMEM((2, xrows, plane), f32),
            pltpu.VMEM((2, yrows, plane), f32),
            pltpu.VMEM((2, xrows, plane), f32),
            pltpu.VMEM((2, yrows, plane), f32),
            sems(2), sems(2), sems(2), sems(2),
            pltpu.VMEM(last.shape, f32),
            pltpu.VMEM((cap, 6 * rhs, cells), bf16),
            pltpu.VMEM((cells, TILE), bf16),
            pltpu.VMEM((rhs, 2 * rhs), f32),
            pltpu.VMEM((n_px, 3 * rhs, width), f32),
            pltpu.VMEM((n_px, rhs, 2 * rhs), f32),
            pltpu.VMEM((n_px, 3 * rhs, width), f32),
            pltpu.VMEM((n_py, rhs, 2 * rhs), f32),
            pltpu.VMEM((n_py, 3 * rhs, width), f32),
            pltpu.VMEM((n_px, 2 * rhs, 3 * rhs), f32),
            sems(n_px), sems(n_px), sems(n_px), sems(n_px),
            sems(n_py), sems(n_py), sems(n_py), sems(n_py),
            sems(n_px), sems(n_px),
        ],
        compiler_params=params(collective_id=0, has_side_effects=True),
    )(counts, last, old, kap, sgn, rows, prev, resid)


def body(
    n_px, n_py, counts, coefficient, signs, basis_old, basis_last, residual_factor, previous_coef,
    sample_rows,
):
    total_cells = MEANX * n_px * n_py * coefficient.shape[2]
    rows = sample_rows.reshape(1, -1)
    return step(
        n_px, n_py, total_cells, counts, basis_last, basis_old, coefficient, signs, rows,
        previous_coef, residual_factor,
    )


def solution(mesh):
    in_specs = (
        P(),
        P("px", "py", None),
        P("px", "py", None),
        P("px", "py", None, None),
        P("px", "py", None, None),
        P(),
        P(),
        P(),
    )
    out_specs = (P("px", "py", None, None), P(None, ("px", "py")), P())
    return jax.shard_map(
        functools.partial(body, mesh.shape["px"], mesh.shape["py"]),
        mesh=mesh,
        in_specs=in_specs,
        out_specs=out_specs,
        check_vma=False,
    )
```

time: 226 us -> 54.5 us (0.24)
  waiting for transfers between devices: 88.3 us -> 0 us
  blocking collectives: 78.2 us -> 0 us
  between operations: 14.1 us -> 0.65 us
  Pallas kernels: 33.4 us -> 43.6 us
    unnamed x2 -> x0, waiting for transfers between devices: 88.3 us -> none
    psum x2 -> x0, blocking collectives: 78.2 us -> none  [the longest x1 41.3 us: body(): proj = lax.psum(gram, ('px', 'py')) / total_cells]
    pallas_call x5 -> x1, Pallas kernels: 33.4 us -> 43.6 us  [step(): pl.pallas_call(functools.partial(step_kernel, n_px, n_py, total_cells), o...]
    unnamed x26 -> x17, local copies, waits for them, and re-layouts: 10.5 us -> 9.17 us
  transfers between devices with their start and end apart: 1 -> 0, of which waited for: 1 -> 0; matrix products, arithmetic and copies ran while one was open for 0% -> 0% of each run, Pallas kernels for 2% -> 0%
where the time goes in v3:
time: 54.5 us; the launch traced here: 54.1 us
  Pallas kernels  43.6 us (80%)
  local copies, waits for them, and re-layouts  9.84 us (18%)
  between operations  0.65 us (1%)
    pallas_call x1, Pallas kernels, step(): pl.pallas_call(functools.partial(step_kernel, n_px, n_py, total_cells), o...  43.6 us
    unnamed x17, local copies, waits for them, and re-layouts  9.17 us

profile of v3, /device:TPU:0, one launch (start us, length us, event | category | flops | bytes accessed | tf_op | source)
XLA Modules:
  0.0 54.1 jit_solution(10726049428931288358)
XLA Ops:
  0.6 0.8 %copy.11.prev_ref = f32[32,16]{1,0:T(8,128)S(1)} copy(f32[32,16]{0,1:T(8,128)} %param.14) | data formatting | bytes 4096 | tf_op args[6]
  1.4 0.0 copy-start
  1.4 1.4 %copy-done = f32[6,1,16,4096]{3,2,1,0:T(8,128)S(1)} copy-done((f32[6,1,16,4096]{3,2,1,0:T(8,128)S(1)}, f32[6,1,16,4096]{3,2,1,0:T(8,128)}, u32[]{:S(2)}) %copy-start) | copy-done | bytes 1572888
  2.8 0.0 copy-start.1
  2.8 1.4 %copy-done.1 = f32[6,1,16,4096]{3,2,1,0:T(8,128)S(1)} copy-done((f32[6,1,16,4096]{3,2,1,0:T(8,128)S(1)}, f32[6,1,16,4096]{3,2,1,0:T(8,128)}, u32[]{:S(2)}) %copy-start.1) | copy-done | bytes 1572888
  4.2 0.0 copy-start.2
  4.2 0.9 %copy-done.2 = f32[6,1,4096]{2,1,0:T(1,128)S(1)} copy-done((f32[6,1,4096]{2,1,0:T(1,128)S(1)}, f32[6,1,4096]{2,1,0:T(1,128)}, u32[]{:S(2)}) %copy-start.2) | copy-done | bytes 98328
  5.1 0.0 copy-start.3
  5.1 0.9 %copy-done.3 = s32[6,1,4096]{2,1,0:T(1,128)S(1)} copy-done((s32[6,1,4096]{2,1,0:T(1,128)S(1)}, s32[6,1,4096]{2,1,0:T(1,128)}, u32[]{:S(2)}) %copy-start.3) | copy-done | bytes 98328
  6.0 0.0 copy-start.4
  6.0 0.7 %copy-done.4 = s32[2048]{0:T(1024)S(1)} copy-done((s32[2048]{0:T(1024)S(1)}, s32[2048]{0:T(1024)}, u32[]{:S(2)}) %copy-start.4) | copy-done | bytes 8216
  6.7 0.0 copy-start.5
  6.7 0.7 %copy-done.5 = f32[16,16]{1,0:T(8,128)S(1)} copy-done((f32[16,16]{1,0:T(8,128)S(1)}, f32[16,16]{1,0:T(8,128)}, u32[]{:S(2)}) %copy-start.5) | copy-done | bytes 1048
  7.4 0.0 copy-start.6
  7.4 0.7 %copy-done.6 = s32[8]{0:T(128)S(1)} copy-done((s32[8]{0:T(128)S(1)}, s32[8]{0:T(128)}, u32[]{:S(2)}) %copy-start.6) | copy-done | bytes 56
  8.1 43.6 %shard_map.103 = (f32[6,1,16,4096]{3,2,1,0:T(8,128)S(1)}, f32[48,64]{1,0:T(8,128)S(1)}, f32[32,16]{1,0:T(8,128)S(1)}) custom-call(s32[8]{0:T(128)S(1)} %copy-done.6, f32[6,1,16,4096]{3,2,1,0:T(8,128)S(1)} %copy-done, f32[6,1,16,4096]{3,2,1,0:T(8,128)S(1)} %copy-done.1, f32[6,1,4096]{2,1,0:T(1,128)S(1)} %copy-done.2, s32[6,1,4096]{2,1,0:T(1,128)S(1)} %copy-done.3, ...), custom_call_target="tpu_custom_call" | custom-call | tf_op jit(solution)/shard_map/pallas_call | solution.py:413
  51.7 0.7 %copy.12 = f32[32,16]{0,1:T(8,128)} copy(f32[32,16]{1,0:T(8,128)S(1)} %get-tuple-element.5) | data formatting | bytes 4096 | tf_op jit(solution)/shard_map/pallas_call | solution.py:413
  52.3 1.1 %copy.15 = f32[6,1,16,4096]{3,2,1,0:T(8,128)} copy(f32[6,1,16,4096]{3,2,1,0:T(8,128)S(1)} %get-tuple-element.9) | data formatting | bytes 3145728
  53.5 0.6 %copy.16 = f32[48,64]{1,0:T(8,128)} copy(f32[48,64]{1,0:T(8,128)S(1)} %get-tuple-element.10) | data formatting | bytes 24576
Async XLA Ops:
  1.4 1.4 %copy-start = (f32[6,1,16,4096]{3,2,1,0:T(8,128)S(1)}, f32[6,1,16,4096]{3,2,1,0:T(8,128)}, u32[]{:S(2)}) copy-start(f32[6,1,16,4096]{3,2,1,0:T(8,128)} %last_hbm.1) | copy-start | bytes 4718596
  2.8 1.4 %copy-start.1 = (f32[6,1,16,4096]{3,2,1,0:T(8,128)S(1)}, f32[6,1,16,4096]{3,2,1,0:T(8,128)}, u32[]{:S(2)}) copy-start(f32[6,1,16,4096]{3,2,1,0:T(8,128)} %old_hbm.1) | copy-start | bytes 4718596
  4.2 0.9 %copy-start.2 = (f32[6,1,4096]{2,1,0:T(1,128)S(1)}, f32[6,1,4096]{2,1,0:T(1,128)}, u32[]{:S(2)}) copy-start(f32[6,1,4096]{2,1,0:T(1,128)} %kap_hbm.1) | copy-start | bytes 294916
  5.1 0.9 %copy-start.3 = (s32[6,1,4096]{2,1,0:T(1,128)S(1)}, s32[6,1,4096]{2,1,0:T(1,128)}, u32[]{:S(2)}) copy-start(s32[6,1,4096]{2,1,0:T(1,128)} %sgn_hbm.1) | copy-start | bytes 294916
  6.0 0.7 %copy-start.4 = (s32[2048]{0:T(1024)S(1)}, s32[2048]{0:T(1024)}, u32[]{:S(2)}) copy-start(s32[2048]{0:T(1024)} %param.15) | copy-start | bytes 24580
  6.7 0.7 %copy-start.5 = (f32[16,16]{1,0:T(8,128)S(1)}, f32[16,16]{1,0:T(8,128)}, u32[]{:S(2)}) copy-start(f32[16,16]{1,0:T(8,128)} %resid_ref.1) | copy-start | bytes 3076
  7.4 0.7 %copy-start.6 = (s32[8]{0:T(128)S(1)}, s32[8]{0:T(128)}, u32[]{:S(2)}) copy-start(s32[8]{0:T(128)} %counts_ref.1) | copy-start | bytes 100

commit v4 on v3

--- a/solution.py
+++ b/solution.py
@@ -20,7 +20,7 @@
 
 
 def params(**more):
-    return pltpu.CompilerParams(vmem_limit_bytes=48 * 1024 * 1024, **more)
+    return pltpu.CompilerParams(vmem_limit_bytes=63 * 1024 * 1024, **more)
 
 
 def parity_sign(values, bits):
@@ -71,7 +71,8 @@
     resid_ref, new_hbm, mine_ref, answer_ref, last_ref, old_ref, kap_ref, sgn_ref, in_sem, out_sem,
     xbuf, ybuf, xg_ref, yg_ref, xsend, xrecv, ysend, yrecv, image_ref, cols, table, gram_ref,
     sketch_ref, gram_x, sketch_x, gram_y, sketch_y, parts_x, gram_xs, gram_xr, sketch_xs,
-    sketch_xr, gram_ys, gram_yr, sketch_ys, sketch_yr, parts_s, parts_r,
+    sketch_xr, gram_ys, gram_yr, sketch_ys, sketch_yr, parts_s, parts_r, table_odd, weights_ref,
+    flips_ref, core_own, core_out, core_in, core_s, core_r,
 ):
     i = lax.axis_index("px")
     j = lax.axis_index("py")
@@ -79,11 +80,15 @@
     plane = PS * PS
     top = (PS - 1) * plane
     mesh_id = pl.DeviceIdType.MESH
+    kap_ref[...] = jnp.zeros(kap_ref.shape, f32)
+    sgn_ref[...] = jnp.zeros(sgn_ref.shape, jnp.int32)
+    pairs = [(last_hbm, last_ref)]
+    pairs += [(kap_hbm.at[s], kap_ref.at[pl.ds(s, 1)]) for s in range(cap)]
+    pairs += [(old_hbm, old_ref)]
+    pairs += [(sgn_hbm.at[s], sgn_ref.at[pl.ds(s, 1)]) for s in range(cap)]
     loads = [
         pltpu.make_async_copy(source, target, in_sem.at[index])
-        for index, (source, target) in enumerate(
-            ((last_hbm, last_ref), (kap_hbm, kap_ref), (old_hbm, old_ref), (sgn_hbm, sgn_ref))
-        )
+        for index, (source, target) in enumerate(pairs)
     ]
     for load in loads:
         load.start()
@@ -108,33 +113,32 @@
         offset = offset + jnp.where(t < i, counts_ref[t], 0)
     tail = jnp.clip(held - 1, 0, cap - 1)
 
-    loads[0].wait()
-    loads[1].wait()
+    for load in loads[:cap + 1]:
+        load.wait()
     xbuf[0, pl.ds(0, rhs), :] = last_ref[0, 0, :, pl.ds(0, plane)]
-    xbuf[0, pl.ds(rhs, 1), :] = kap_ref[0, :, pl.ds(0, plane)]
+    xbuf[0, pl.ds(rhs, 1), :] = kap_ref[pl.ds(0, 1), pl.ds(0, plane)]
     xbuf[1, pl.ds(0, rhs), :] = last_ref[tail, 0, :, pl.ds(top, plane)]
-    xbuf[1, pl.ds(rhs, 1), :] = kap_ref[tail, :, pl.ds(top, plane)]
-
-    def pack(s, carry):
-        u0 = jnp.zeros((rhs, plane), f32)
-        u1 = jnp.zeros((rhs, plane), f32)
-        k0 = jnp.zeros((1, plane), f32)
-        k1 = jnp.zeros((1, plane), f32)
+    xbuf[1, pl.ds(rhs, 1), :] = kap_ref[pl.ds(tail, 1), pl.ds(top, plane)]
+
+    def gather_faces(plane_at, shape):
+        low = jnp.zeros(shape, f32)
+        high = jnp.zeros(shape, f32)
         for a in range(PS):
-            mine = b_id == a
-            u = last_ref[s, 0, :, pl.ds(a * plane, plane)]
-            k = kap_ref[s, :, pl.ds(a * plane, plane)]
+            value = plane_at(pl.ds(a * plane, plane))
             lo = (a * PS) % plane
             hi = (a * PS + PS) % plane
-            u0 = jnp.where(mine, pltpu.roll(u, lo, 1) if lo else u, u0)
-            u1 = jnp.where(mine, pltpu.roll(u, hi, 1) if hi else u, u1)
-            k0 = jnp.where(mine, pltpu.roll(k, lo, 1) if lo else k, k0)
-            k1 = jnp.where(mine, pltpu.roll(k, hi, 1) if hi else k, k1)
-        ybuf[0, pl.ds(pl.multiple_of(s * rhs, 8), rhs), :] = u0
-        ybuf[1, pl.ds(pl.multiple_of(s * rhs, 8), rhs), :] = u1
-        ybuf[0, pl.ds(cap * rhs + s, 1), :] = k0
-        ybuf[1, pl.ds(cap * rhs + s, 1), :] = k1
+            low = jnp.where(b_id == a, pltpu.roll(value, lo, 1) if lo else value, low)
+            high = jnp.where(b_id == a, pltpu.roll(value, hi, 1) if hi else value, high)
+        return low, high
+
+    def pack(s, carry):
+        low, high = gather_faces(lambda at: last_ref[s, 0, :, at], (rhs, plane))
+        ybuf[0, pl.ds(pl.multiple_of(s * rhs, 8), rhs), :] = low
+        ybuf[1, pl.ds(pl.multiple_of(s * rhs, 8), rhs), :] = high
         return carry
+
+    slots = kap_ref.shape[0]
+    kappa_rows = pl.ds(cap * rhs, slots)
 
     faces = {0: (ybuf, yg_ref, ysend, yrecv), 2: (xbuf, xg_ref, xsend, xrecv)}
 
@@ -158,6 +162,9 @@
     pl.semaphore_wait(barrier, n_px + n_py - 2)
     for side in range(2):
         when_near(2, side, lambda: face_copy(2, side, 1 - side).start())
+    ybuf[0, kappa_rows, :], ybuf[1, kappa_rows, :] = gather_faces(
+        lambda at: kap_ref[:, at], (slots, plane)
+    )
     lax.fori_loop(0, cap, pack, 0)
     for side in range(2):
         when_near(0, side, lambda: face_copy(0, side, 1 - side).start())
@@ -168,11 +175,13 @@
                 ghost = faces[base][1]
                 ghost[side] = jnp.zeros(ghost.shape[1:], f32)
 
-    loads[2].wait()
-    loads[3].wait()
+    for load in loads[cap + 1:]:
+        load.wait()
+    slot_id = lax.broadcasted_iota(jnp.int32, (slots, 1), 0)
+    flips_ref[...] = jnp.where(slot_id < held, 1 - 2 * sgn_ref[...], 0).astype(f32)
 
     def flips(s, at):
-        return jnp.where(s < held, 1 - 2 * sgn_ref[s, :, at], 0).astype(f32)
+        return flips_ref[pl.ds(s, 1), at]
 
     def keep(s, part, at, value):
         first_part, rest = split(value)
@@ -194,61 +203,80 @@
             when_near(base, side, lambda: face_copy(base, side, 1 - side).wait_send())
             when_near(base, side, lambda: face_copy(base, side, side).wait_recv())
 
+    def rolled(value, glo, ghi, a):
+        lo = (plane - a * PS) % plane
+        hi = (plane - PS - a * PS) % plane
+        blo = jnp.where(
+            b_id == 0, pltpu.roll(glo, lo, 1) if lo else glo, pltpu.roll(value, PS, 1)
+        )
+        bhi = jnp.where(
+            b_id == PS - 1,
+            pltpu.roll(ghi, hi, 1) if hi else ghi,
+            pltpu.roll(value, plane - PS, 1),
+        )
+        return blo, bhi, pltpu.roll(value, 1, 1), pltpu.roll(value, plane - 1, 1)
+
+    kg_lo, kg_hi = yg_ref[0, kappa_rows, :], yg_ref[1, kappa_rows, :]
+    for a in range(PS):
+        at = pl.ds(a * plane, plane)
+        k = kap_ref[:, at]
+        if a == 0:
+            below = jnp.where(
+                slot_id == 0,
+                xg_ref[0, pl.ds(rhs, 1), :],
+                pltpu.roll(kap_ref[:, pl.ds(top, plane)], 1, 0),
+            )
+        else:
+            below = kap_ref[:, pl.ds((a - 1) * plane, plane)]
+        if a == PS - 1:
+            above = jnp.where(
+                slot_id == held - 1,
+                xg_ref[1, pl.ds(rhs, 1), :],
+                pltpu.roll(kap_ref[:, pl.ds(0, plane)], slots - 1, 0),
+            )
+        else:
+            above = kap_ref[:, pl.ds((a + 1) * plane, plane)]
+        kr = rolled(k, kg_lo, kg_hi, a)
+        ends = (c_id == 0, c_id == PS - 1)
+        near = (below, above, kr[0], kr[1]) + tuple(
+            jnp.where(end, 0.0, kn) for end, kn in zip(ends, kr[2:])
+        )
+        weights = [0.5 * (k + kn) for kn in near]
+        diag = weights[0]
+        for w in weights[1:]:
+            diag = diag + w
+        weights[4] = jnp.where(ends[0], 0.0, weights[4])
+        weights[5] = jnp.where(ends[1], 0.0, weights[5])
+        for n, w in enumerate(weights + [diag]):
+            weights_ref[n, :, at] = w
+
     def operate(s, carry):
         live = s < held
-        first = s == 0
-        final = s == held - 1
         before = jnp.maximum(s - 1, 0)
         after = jnp.minimum(s + 1, cap - 1)
-        ks = pl.ds(cap * rhs + s, 1)
         us = pl.ds(pl.multiple_of(s * rhs, 8), rhs)
-        kg_lo, kg_hi = yg_ref[0, ks, :], yg_ref[1, ks, :]
         ug_lo, ug_hi = yg_ref[0, us, :], yg_ref[1, us, :]
         for a in range(PS):
             at = pl.ds(a * plane, plane)
-
-            def planes(ref_at, ghost_rows):
-                if a == 0:
-                    low = jnp.where(first, xg_ref[0, ghost_rows, :], ref_at(before, top))
-                else:
-                    low = ref_at(s, (a - 1) * plane)
-                if a == PS - 1:
-                    high = jnp.where(final, xg_ref[1, ghost_rows, :], ref_at(after, 0))
-                else:
-                    high = ref_at(s, (a + 1) * plane)
-                return low, high
-
-            def rolled(value, glo, ghi):
-                lo = (plane - a * PS) % plane
-                hi = (plane - PS - a * PS) % plane
-                blo = jnp.where(
-                    b_id == 0, pltpu.roll(glo, lo, 1) if lo else glo, pltpu.roll(value, PS, 1)
+            u = last_ref[s, 0, :, at]
+            if a == 0:
+                low = jnp.where(
+                    s == 0, xg_ref[0, pl.ds(0, rhs), :], last_ref[before, 0, :, pl.ds(top, plane)]
                 )
-                bhi = jnp.where(
-                    b_id == PS - 1,
-                    pltpu.roll(ghi, hi, 1) if hi else ghi,
-                    pltpu.roll(value, plane - PS, 1),
+            else:
+                low = last_ref[s, 0, :, pl.ds((a - 1) * plane, plane)]
+            if a == PS - 1:
+                high = jnp.where(
+                    s == held - 1,
+                    xg_ref[1, pl.ds(0, rhs), :],
+                    last_ref[after, 0, :, pl.ds(0, plane)],
                 )
-                return blo, bhi, pltpu.roll(value, 1, 1), pltpu.roll(value, plane - 1, 1)
-
-            k = kap_ref[s, :, at]
-            u = last_ref[s, 0, :, at]
-            ka = planes(lambda t, p: kap_ref[t, :, pl.ds(p, plane)], pl.ds(rhs, 1))
-            ua = planes(lambda t, p: last_ref[t, 0, :, pl.ds(p, plane)], pl.ds(0, rhs))
-            kr = rolled(k, kg_lo, kg_hi)
-            ur = rolled(u, ug_lo, ug_hi)
-            kc = (jnp.where(c_id == 0, 0.0, kr[2]), jnp.where(c_id == PS - 1, 0.0, kr[3]))
-            near_k = (ka[0], ka[1], kr[0], kr[1], kc[0], kc[1])
-            near_u = (ua[0], ua[1]) + ur
-            weights = [0.5 * (k + kn) for kn in near_k]
-            diag = weights[0]
-            for w in weights[1:]:
-                diag = diag + w
-            weights[4] = jnp.where(c_id == 0, 0.0, weights[4])
-            weights[5] = jnp.where(c_id == PS - 1, 0.0, weights[5])
-            image = diag * u
-            for w, un in zip(weights, near_u):
-                image = image - w * un
+            else:
+                high = last_ref[s, 0, :, pl.ds((a + 1) * plane, plane)]
+            near = (low, high) + rolled(u, ug_lo, ug_hi, a)
+            image = weights_ref[6, pl.ds(s, 1), at] * u
+            for n, un in enumerate(near):
+                image = image - weights_ref[n, pl.ds(s, 1), at] * un
             image = jnp.where(live, image, 0.0)
             image_ref[s, 0, :, at] = image
             keep(s, 2, at, image * flips(s, at))
@@ -314,18 +342,53 @@
     tiles = rows_ref.shape[1] // TILE
     scale = 1.0 / math.sqrt(total_cells)
 
-    def one_tile(turn, carry):
-        t = lax.rem(i // per + 1 + turn, tiles)
-        at = pl.ds(pl.multiple_of(t * TILE, TILE), TILE)
-        rows = rows_ref[:, at]
+    core = lax.rem(j, 2)
+    partner = j + 1 - 2 * core
+    half_rows = 3 * rhs // 2
+
+    def tile_of(turn):
+        return lax.rem(i // per + 1 + turn, tiles)
+
+    def rows_of(turn):
+        return rows_ref[:, pl.ds(pl.multiple_of(tile_of(turn) * TILE, TILE), TILE)]
+
+    def fill(signs_of, turn):
+        rows = rows_of(turn)
         inside = parity_sign(jnp.bitwise_and(inner, rows), 8).astype(f32).astype(bf16)
         across = parity_sign(
             jnp.bitwise_and(hi_ids, jnp.right_shift(rows, 8) & (outer - 1)), 4
         ).astype(f32)
         for h in range(outer):
-            table[pl.ds(h * TILE, TILE), :] = inside * across[h:h + 1].astype(bf16)
+            signs_of[pl.ds(h * TILE, TILE), :] = inside * across[h:h + 1].astype(bf16)
+
+    def spread_of(signs_of):
         flat = cols[...].reshape(cap * 6 * rhs, cells)
-        spread = jnp.dot(flat, table[...], preferred_element_type=f32)
+        return jnp.dot(flat, signs_of[...], preferred_element_type=f32)
+
+    def core_copy(turn):
+        return pltpu.make_async_remote_copy(
+            src_ref=core_out.at[turn],
+            dst_ref=core_in.at[turn],
+            send_sem=core_s.at[turn],
+            recv_sem=core_r.at[turn],
+            device_id={"py": partner},
+            device_id_type=mesh_id,
+        )
+
+    def forward(turn):
+        core_copy(turn).wait_recv()
+        block = core_own[turn] + core_in[turn]
+        t = tile_of(turn)
+        for r in range(per):
+            owner = t * per + r
+            sketch_ref[owner] = block[:, r * width:(r + 1) * width]
+
+            @pl.when(owner != i)
+            def _():
+                sketch_x_copy(owner, i).start()
+
+    def emit(turn, spread):
+        rows = rows_of(turn)
         summed = jnp.zeros((3 * rhs, TILE), f32)
         for s in range(cap):
             patch = (offset + s) * n_py + j
@@ -337,21 +400,31 @@
                 spread[base:base + 3 * rhs] + spread[base + 3 * rhs:base + 6 * rhs]
             )
         summed = summed * scale
-        for r in range(per):
-            owner = t * per + r
-            sketch_ref[owner] = summed[:, r * width:(r + 1) * width]
-
-            @pl.when(owner != i)
-            def _():
-                sketch_x_copy(owner, i).start()
+        core_own[turn] = jnp.where(core == 0, summed[:half_rows], summed[half_rows:])
+        core_out[turn] = jnp.where(core == 0, summed[half_rows:], summed[:half_rows])
+        core_copy(turn).start()
+
+        @pl.when(turn > 0)
+        def _():
+            forward(turn - 1)
+
+    def two_tiles(pair_id, carry):
+        turn = 2 * pair_id
+        fill(table_odd, turn + 1)
+        spread = spread_of(table)
+        emit(turn, spread)
+        fill(table, turn + 2)
+        spread = spread_of(table_odd)
+        emit(turn + 1, spread)
         return carry
 
-    half = tiles // 2
-    lax.fori_loop(0, half, one_tile, 0)
+    fill(table, 0)
+    lax.fori_loop(0, tiles // 4, two_tiles, 0)
     finish(gram_x_copy, i, x_peers)
     gram_y[j] = total(gram_x)
     start(gram_y_copy, j, y_peers)
-    lax.fori_loop(half, tiles, one_tile, 0)
+    lax.fori_loop(tiles // 4, tiles // 2, two_tiles, 0)
+    forward(tiles - 1)
     sketch_x[i] = sketch_ref[i]
     finish(gram_y_copy, j, y_peers)
     proj = total(gram_y) * (1.0 / total_cells)
@@ -381,10 +454,16 @@
 
     lax.fori_loop(0, cap // 2, one_block, 0)
     finish(sketch_y_copy, j, y_peers)
-    whole = total(sketch_y)
+    halves = []
+    for c in range(2):
+        acc = sketch_y[c]
+        for p in range(c + 2, n_py, 2):
+            acc = acc + sketch_y[p]
+        halves.append(acc)
+    whole = jnp.concatenate(halves, axis=0)
     pair = whole[:2 * rhs]
     second = whole[2 * rhs:]
-    images = jnp.concatenate([tn(prev_ref[...], pair), second], axis=0)
+    images = jnp.concatenate([nn(prev_ref[...], pair), second], axis=0)
     target = tn(resid_ref[...], pair[:rhs])
     parts_x[i] = nt(images, jnp.concatenate([images, target], axis=0))
     start(parts_copy, i, x_peers)
@@ -397,7 +476,9 @@
     ).astype(f32)
     mine_ref[...] = nn(jnp.concatenate([pair, newer], axis=0), chosen)
     finish(parts_copy, i, x_peers)
-    answer_ref[...] = eliminate(total(parts_x))[:, 2 * rhs:]
+    answer_ref[...] = eliminate(total(parts_x))[:, 2 * rhs:].T
+    for turn in range(tiles):
+        core_copy(turn).wait_send()
     for s in range(cap):
         store_of(s).wait()
 
@@ -406,7 +487,10 @@
     cap, _, rhs, cells = last.shape
     width = rows.shape[1] // n_px
     plane = PS * PS
-    yrows = cap * rhs + -(-cap // 8) * 8
+    slots = -(-cap // 8) * 8
+    yrows = cap * rhs + slots
+    tiles = rows.shape[1] // TILE
+    half = 3 * rhs // 2
     xrows = rhs + 8
     hbm = pl.BlockSpec(memory_space=pl.ANY)
     sems = lambda n: pltpu.SemaphoreType.DMA((n,))
@@ -415,16 +499,16 @@
         out_shape=(
             jax.ShapeDtypeStruct(last.shape, f32),
             jax.ShapeDtypeStruct((3 * rhs, width // n_py), f32),
-            jax.ShapeDtypeStruct((2 * rhs, rhs), f32),
+            jax.ShapeDtypeStruct((rhs, 2 * rhs), f32),
         ),
         in_specs=[SMEM] + [hbm] * 4 + [VMEM] * 3,
         out_specs=(hbm, VMEM, VMEM),
         scratch_shapes=[
             pltpu.VMEM(last.shape, f32),
             pltpu.VMEM(old.shape, f32),
-            pltpu.VMEM(kap.shape, f32),
-            pltpu.VMEM(sgn.shape, jnp.int32),
-            sems(4), sems(cap),
+            pltpu.VMEM((slots, cells), f32),
+            pltpu.VMEM((slots, cells), jnp.int32),
+            sems(2 + 2 * cap), sems(cap),
             pltpu.VMEM((2, xrows, plane), f32),
             pltpu.VMEM((2, yrows, plane), f32),
             pltpu.VMEM((2, xrows, plane), f32),
@@ -434,15 +518,22 @@
             pltpu.VMEM((cap, 6 * rhs, cells), bf16),
             pltpu.VMEM((cells, TILE), bf16),
             pltpu.VMEM((rhs, 2 * rhs), f32),
-            pltpu.VMEM((n_px, 3 * rhs, width), f32),
+            pltpu.VMEM((n_px, half, width), f32),
             pltpu.VMEM((n_px, rhs, 2 * rhs), f32),
-            pltpu.VMEM((n_px, 3 * rhs, width), f32),
+            pltpu.VMEM((n_px, half, width), f32),
             pltpu.VMEM((n_py, rhs, 2 * rhs), f32),
-            pltpu.VMEM((n_py, 3 * rhs, width), f32),
+            pltpu.VMEM((n_py, half, width), f32),
             pltpu.VMEM((n_px, 2 * rhs, 3 * rhs), f32),
             sems(n_px), sems(n_px), sems(n_px), sems(n_px),
             sems(n_py), sems(n_py), sems(n_py), sems(n_py),
             sems(n_px), sems(n_px),
+            pltpu.VMEM((cells, TILE), bf16),
+            pltpu.VMEM((7, slots, cells), f32),
+            pltpu.VMEM((slots, cells), f32),
+            pltpu.VMEM((tiles, half, TILE), f32),
+            pltpu.VMEM((tiles, half, TILE), f32),
+            pltpu.VMEM((tiles, half, TILE), f32),
+            sems(tiles), sems(tiles),
         ],
         compiler_params=params(collective_id=0, has_side_effects=True),
     )(counts, last, old, kap, sgn, rows, prev, resid)
@@ -454,10 +545,11 @@
 ):
     total_cells = MEANX * n_px * n_py * coefficient.shape[2]
     rows = sample_rows.reshape(1, -1)
-    return step(
+    new_block, mine, answer = step(
         n_px, n_py, total_cells, counts, basis_last, basis_old, coefficient, signs, rows,
-        previous_coef, residual_factor,
-    )
+        previous_coef.T, residual_factor,
+    )
+    return (new_block, mine, answer.T)
 
 
 def solution(mesh):

time: 54.5 us -> 60.2 us (1.10)
  Pallas kernels: 43.6 us -> 55.4 us
  local copies, waits for them, and re-layouts: 9.84 us -> 3.88 us
    pallas_call x1, Pallas kernels: 43.6 us -> 55.4 us  [step(): pl.pallas_call(functools.partial(step_kernel, n_px, n_py, total_cells), o...]
    unnamed x17 -> x7, local copies, waits for them, and re-layouts: 9.17 us -> 3.88 us
    pallas_call x1 -> x0, local copies, waits for them, and re-layouts: 0.67 us -> none  [step(): pl.pallas_call(functools.partial(step_kernel, n_px, n_py, total_cells), o...]
where the time goes in v4:
time: 60.2 us; the launch traced here: 60 us
  Pallas kernels  55.4 us (92%)
  local copies, waits for them, and re-layouts  3.88 us (6%)
  between operations  0.66 us (1%)
    pallas_call x1, Pallas kernels, step(): pl.pallas_call(functools.partial(step_kernel, n_px, n_py, total_cells), o...  55.4 us
    unnamed x7, local copies, waits for them, and re-layouts  3.88 us

profile of v4, /device:TPU:0, one launch (start us, length us, event | category | flops | bytes accessed | tf_op | source)
XLA Modules:
  0.0 60.0 jit_solution(9413479255847035259)
XLA Ops:
  0.6 55.4 %shard_map.103 = (f32[6,1,16,4096]{3,2,1,0:T(8,128)}, f32[48,64]{1,0:T(8,128)}, f32[16,32]{1,0:T(8,128)}) custom-call(s32[8]{0:T(128)} %counts_ref.1, f32[6,1,16,4096]{3,2,1,0:T(8,128)} %last_hbm.1, f32[6,1,16,4096]{3,2,1,0:T(8,128)} %old_hbm.1, f32[6,1,4096]{2,1,0:T(1,128)} %kap_hbm.1, s32[6,1,4096]{2,1,0:T(1,128)} %sgn_hbm.1, s32[1,2048]{1,0:T(1,128)} %bitcast.3, ...), custom_call_target="tpu_custom_call" | custom-call | tf_op jit(solution)/shard_map/pallas_call | solution.py:497
  56.1 0.0 copy-start
  56.1 0.0 copy-start.1
  56.1 2.7 %copy.14 = f32[6,1,16,4096]{3,2,1,0:T(8,128)} copy(f32[6,1,16,4096]{3,2,1,0:T(8,128)} %get-tuple-element.12) | data formatting | bytes 3145728
  58.8 0.0 copy-done
  58.8 0.6 %copy.15 = f32[48,64]{1,0:T(8,128)} copy(f32[48,64]{1,0:T(8,128)S(1)} %copy-done) | data formatting | bytes 24576
  59.4 0.0 copy-done.1
  59.4 0.6 copy.16
Async XLA Ops:
  56.1 2.7 %copy-start = (f32[48,64]{1,0:T(8,128)S(1)}, f32[48,64]{1,0:T(8,128)}, u32[]{:S(2)}) copy-start(f32[48,64]{1,0:T(8,128)} %get-tuple-element.13) | copy-start | bytes 36868
  56.1 3.3 %copy-start.1 = (f32[16,32]{1,0:T(8,128)S(1)}, f32[16,32]{1,0:T(8,128)}, u32[]{:S(2)}) copy-start(f32[16,32]{1,0:T(8,128)} %get-tuple-element.8) | copy-start | bytes 6148

commit v5 on v4

--- a/solution.py
+++ b/solution.py
@@ -71,7 +71,7 @@
     resid_ref, new_hbm, mine_ref, answer_ref, last_ref, old_ref, kap_ref, sgn_ref, in_sem, out_sem,
     xbuf, ybuf, xg_ref, yg_ref, xsend, xrecv, ysend, yrecv, image_ref, cols, table, gram_ref,
     sketch_ref, gram_x, sketch_x, gram_y, sketch_y, parts_x, gram_xs, gram_xr, sketch_xs,
-    sketch_xr, gram_ys, gram_yr, sketch_ys, sketch_yr, parts_s, parts_r, table_odd, weights_ref,
+    sketch_xr, gram_ys, gram_yr, sketch_ys, sketch_yr, parts_s, parts_r, weights_ref,
     flips_ref, core_own, core_out, core_in, core_s, core_r,
 ):
     i = lax.axis_index("px")
@@ -408,22 +408,17 @@
         def _():
             forward(turn - 1)
 
-    def two_tiles(pair_id, carry):
-        turn = 2 * pair_id
-        fill(table_odd, turn + 1)
-        spread = spread_of(table)
-        emit(turn, spread)
-        fill(table, turn + 2)
-        spread = spread_of(table_odd)
-        emit(turn + 1, spread)
+    def one_tile(turn, carry):
+        fill(table, turn)
+        emit(turn, spread_of(table))
         return carry
 
-    fill(table, 0)
-    lax.fori_loop(0, tiles // 4, two_tiles, 0)
+    half = tiles // 2
+    lax.fori_loop(0, half, one_tile, 0)
     finish(gram_x_copy, i, x_peers)
     gram_y[j] = total(gram_x)
     start(gram_y_copy, j, y_peers)
-    lax.fori_loop(tiles // 4, tiles // 2, two_tiles, 0)
+    lax.fori_loop(half, tiles, one_tile, 0)
     forward(tiles - 1)
     sketch_x[i] = sketch_ref[i]
     finish(gram_y_copy, j, y_peers)
@@ -527,7 +522,6 @@
             sems(n_px), sems(n_px), sems(n_px), sems(n_px),
             sems(n_py), sems(n_py), sems(n_py), sems(n_py),
             sems(n_px), sems(n_px),
-            pltpu.VMEM((cells, TILE), bf16),
             pltpu.VMEM((7, slots, cells), f32),
             pltpu.VMEM((slots, cells), f32),
             pltpu.VMEM((tiles, half, TILE), f32),

time: 60.2 us -> 49.2 us (0.82)
  Pallas kernels: 55.4 us -> 44.5 us
    pallas_call x1, Pallas kernels: 55.4 us -> 44.5 us  [step(): pl.pallas_call(functools.partial(step_kernel, n_px, n_py, total_cells), o...]
where the time goes in v5:
time: 49.2 us; the launch traced here: 49 us
  Pallas kernels  44.5 us (90%)
  local copies, waits for them, and re-layouts  3.88 us (8%)
  between operations  0.66 us (1%)
    pallas_call x1, Pallas kernels, step(): pl.pallas_call(functools.partial(step_kernel, n_px, n_py, total_cells), o...  44.5 us
    unnamed x7, local copies, waits for them, and re-layouts  3.88 us

profile of v5, /device:TPU:0, one launch (start us, length us, event | category | flops | bytes accessed | tf_op | source)
XLA Modules:
  0.0 49.0 jit_solution(16914862075369104840)
XLA Ops:
  0.6 44.5 %shard_map.103 = (f32[6,1,16,4096]{3,2,1,0:T(8,128)}, f32[48,64]{1,0:T(8,128)}, f32[16,32]{1,0:T(8,128)}) custom-call(s32[8]{0:T(128)} %counts_ref.1, f32[6,1,16,4096]{3,2,1,0:T(8,128)} %last_hbm.1, f32[6,1,16,4096]{3,2,1,0:T(8,128)} %old_hbm.1, f32[6,1,4096]{2,1,0:T(1,128)} %kap_hbm.1, s32[6,1,4096]{2,1,0:T(1,128)} %sgn_hbm.1, s32[1,2048]{1,0:T(1,128)} %bitcast.3, ...), custom_call_target="tpu_custom_call" | custom-call | tf_op jit(solution)/shard_map/pallas_call | solution.py:492
  45.1 0.0 copy-start
  45.1 0.0 copy-start.1
  45.2 2.7 %copy.14 = f32[6,1,16,4096]{3,2,1,0:T(8,128)} copy(f32[6,1,16,4096]{3,2,1,0:T(8,128)} %get-tuple-element.12) | data formatting | bytes 3145728
  47.8 0.0 copy-done
  47.8 0.6 %copy.15 = f32[48,64]{1,0:T(8,128)} copy(f32[48,64]{1,0:T(8,128)S(1)} %copy-done) | data formatting | bytes 24576
  48.4 0.0 copy-done.1
  48.4 0.6 %copy.16 = f32[32,16]{0,1:T(8,128)} copy(f32[32,16]{0,1:T(8,128)S(1)} %bitcast.5) | data formatting | bytes 4096
Async XLA Ops:
  45.1 2.7 %copy-start = (f32[48,64]{1,0:T(8,128)S(1)}, f32[48,64]{1,0:T(8,128)}, u32[]{:S(2)}) copy-start(f32[48,64]{1,0:T(8,128)} %get-tuple-element.13) | copy-start | bytes 36868
  45.1 3.3 %copy-start.1 = (f32[16,32]{1,0:T(8,128)S(1)}, f32[16,32]{1,0:T(8,128)}, u32[]{:S(2)}) copy-start(f32[16,32]{1,0:T(8,128)} %get-tuple-element.8) | copy-start | bytes 6148

commit v6 on v5

--- a/solution.py
+++ b/solution.py
@@ -53,12 +53,19 @@
 def eliminate(work):
     size, width = work.shape
     row_id = lax.broadcasted_iota(jnp.int32, (size, 1), 0)
-    for step in range(size):
-        row = work[step:step + 1, :]
-        pivot = row[:, step:step + 1]
-        scaled = row / pivot
-        column = jnp.where(row_id == step, 0.0, work[:, step:step + 1])
-        work = jnp.where(row_id == step, scaled, work - column * scaled)
+    for step in range(0, size, 2):
+        row0 = work[step:step + 1, :]
+        row1 = work[step + 1:step + 2, :]
+        col0 = work[:, step:step + 1]
+        col1 = work[:, step + 1:step + 2]
+        inv0 = 1.0 / row0[:, step:step + 1]
+        ratio = row1[:, step:step + 1] * inv0
+        left = row0[:, step + 1:step + 2]
+        inv1 = 1.0 / (row1[:, step + 1:step + 2] - ratio * left)
+        new1 = (row1 - ratio * row0) * inv1
+        new0 = (row0 - left * new1) * inv0
+        rest = work - col0 * new0 - col1 * new1
+        work = jnp.where(row_id == step, new0, jnp.where(row_id == step + 1, new1, rest))
     return work
 
 
@@ -188,15 +195,18 @@
         cols[s, pl.ds(part * rhs, rhs), at] = first_part
         cols[s, pl.ds((part + 3) * rhs, rhs), at] = rest
 
-    def pair_columns(s, carry):
-        for a in range(PS):
-            at = pl.ds(a * plane, plane)
-            sg = flips(s, at)
-            keep(s, 0, at, old_ref[s, 0, :, at] * sg)
-            keep(s, 1, at, last_ref[s, 0, :, at] * sg)
+    chunk = 4 * plane
+    chunks = cells // chunk
+
+    def pair_columns(index, carry):
+        s = index // chunks
+        at = pl.ds(pl.multiple_of(lax.rem(index, chunks) * chunk, chunk), chunk)
+        sg = flips(s, at)
+        keep(s, 0, at, old_ref[s, 0, :, at] * sg)
+        keep(s, 1, at, last_ref[s, 0, :, at] * sg)
         return carry
 
-    lax.fori_loop(0, cap, pair_columns, 0)
+    lax.fori_loop(0, cap * chunks, pair_columns, 0)
 
     for base in (2, 0):
         for side in range(2):
@@ -533,6 +543,32 @@
     )(counts, last, old, kap, sgn, rows, prev, resid)
 
 
+def place_kernel(new_ref, mine_ref, answer_ref, new_out, mine_out, answer_out, sems):
+    cap = new_ref.shape[0]
+    moves = [(mine_ref, mine_out), (answer_ref, answer_out)]
+    moves += [(new_ref.at[s], new_out.at[s]) for s in range(cap)]
+    copies = [
+        pltpu.make_async_copy(source, target, sems.at[n])
+        for n, (source, target) in enumerate(moves)
+    ]
+    for copy in copies:
+        copy.start()
+    for copy in copies:
+        copy.wait()
+
+
+def place(*arrays):
+    hbm = pl.BlockSpec(memory_space=pl.ANY)
+    return pl.pallas_call(
+        place_kernel,
+        out_shape=tuple(jax.ShapeDtypeStruct(a.shape, f32) for a in arrays),
+        in_specs=[hbm] * 3,
+        out_specs=(hbm,) * 3,
+        scratch_shapes=[pltpu.SemaphoreType.DMA((2 + arrays[0].shape[0],))],
+        compiler_params=params(),
+    )(*arrays)
+
+
 def body(
     n_px, n_py, counts, coefficient, signs, basis_old, basis_last, residual_factor, previous_coef,
     sample_rows,
@@ -543,6 +579,7 @@
         n_px, n_py, total_cells, counts, basis_last, basis_old, coefficient, signs, rows,
         previous_coef.T, residual_factor,
     )
+    new_block, mine, answer = place(new_block, mine, answer)
     return (new_block, mine, answer.T)
 
 

time: 49.2 us -> 96.1 us (1.95)
  Pallas kernels: 44.5 us -> 95.3 us
  local copies, waits for them, and re-layouts: 3.88 us -> 0 us
    pallas_call x0 -> x1, Pallas kernels: none -> 49.8 us  [place(): pl.pallas_call(place_kernel, out_shape=tuple((jax.ShapeDtypeStruct(a.shap...]
    unnamed x7 -> x0, local copies, waits for them, and re-layouts: 3.88 us -> none
    pallas_call x1, Pallas kernels: 44.5 us -> 45.5 us  [step(): pl.pallas_call(functools.partial(step_kernel, n_px, n_py, total_cells), o...]
where the time goes in v6:
time: 96.1 us; the launch traced here: 95.9 us
  Pallas kernels  95.3 us (99%)
    pallas_call x1, Pallas kernels, place(): pl.pallas_call(place_kernel, out_shape=tuple((jax.ShapeDtypeStruct(a.shap...  49.8 us
    pallas_call x1, Pallas kernels, step(): pl.pallas_call(functools.partial(step_kernel, n_px, n_py, total_cells), o...  45.5 us

profile of v6, /device:TPU:0, one launch (start us, length us, event | category | flops | bytes accessed | tf_op | source)
XLA Modules:
  0.0 95.9 jit_solution(1196339804866999593)
XLA Ops:
  0.6 45.5 %shard_map.103 = (f32[6,1,16,4096]{3,2,1,0:T(8,128)}, f32[48,64]{1,0:T(8,128)}, f32[16,32]{1,0:T(8,128)}) custom-call(s32[8]{0:T(128)} %counts_ref.1, f32[6,1,16,4096]{3,2,1,0:T(8,128)} %last_hbm.1, f32[6,1,16,4096]{3,2,1,0:T(8,128)} %old_hbm.1, f32[6,1,4096]{2,1,0:T(1,128)} %kap_hbm.1, s32[6,1,4096]{2,1,0:T(1,128)} %sgn_hbm.1, s32[1,2048]{1,0:T(1,128)} %bitcast.3, ...), custom_call_target="tpu_custom_call" | custom-call | tf_op jit(solution)/shard_map/pallas_call | solution.py:502
  46.1 49.8 %shard_map.104 = (f32[6,1,16,4096]{3,2,1,0:T(8,128)}, f32[48,64]{1,0:T(8,128)}, f32[16,32]{1,0:T(8,128)}) custom-call(f32[6,1,16,4096]{3,2,1,0:T(8,128)} %get-tuple-element.9.new_ref, f32[48,64]{1,0:T(8,128)} %get-tuple-element.10.mine_ref, f32[16,32]{1,0:T(8,128)} %get-tuple-element.11.answer_ref), custom_call_target="tpu_custom_call" | custom-call | tf_op jit(solution)/shard_map/pallas_call | solution.py:562
